TPU v7x, 32 devices: a whole 2x2x4 slice. The times are simulated.
32 devices in a mesh: dp: 16 (over z, y, x), tp: 2 (over core).
Axes of the slice: x: 2, y: 2, z: 4, core: 2. Of those that a mesh axis runs over, the one named last changes fastest.
Arguments:
- x_visible: bfloat16 [25088, 384], P('dp'), may hold values from -6 to 6
- patch_order: int32 [256, 196], P('dp'), may hold values from 0 to 195, each once within a row
- enc_qkv: bfloat16 [3, 384, 384], P(None, None, 'tp'), may hold values from -0.3125 to 0.3125
- enc_head_bias: float32 [2, 384], P(None, 'tp'), may hold values from -1.8 to 1.8
- enc_proj: bfloat16 [384, 384], P('tp'), may hold values from -1.25 to 1.25
- enc_fc1: bfloat16 [384, 1536], P(None, 'tp'), may hold values from -0.3125 to 0.3125
- enc_fc1_bias: float32 [1536], P('tp'), may hold values from -1.8 to 1.8
- enc_fc2: bfloat16 [1536, 384], P('tp'), may hold values from -0.15625 to 0.15625
- enc_gains: float32 [4, 384], replicated, may hold values from 0.25 to 1.75
- enc_shifts: float32 [4, 384], replicated, may hold values from -1.8 to 1.8
- reg_qkv: bfloat16 [3, 384, 384], P(None, None, 'tp'), may hold values from -0.3125 to 0.3125
- reg_head_bias: float32 [2, 384], P(None, 'tp'), may hold values from -1.8 to 1.8
- reg_proj: bfloat16 [384, 384], P('tp'), may hold values from -1.25 to 1.25
- reg_fc1: bfloat16 [384, 1536], P(None, 'tp'), may hold values from -0.3125 to 0.3125
- reg_fc1_bias: float32 [1536], P('tp'), may hold values from -1.8 to 1.8
- reg_fc2: bfloat16 [1536, 384], P('tp'), may hold values from -0.15625 to 0.15625
- reg_gains: float32 [5, 384], replicated, may hold values from 0.25 to 1.75
- reg_shifts: float32 [5, 384], replicated, may hold values from -1.8 to 1.8
- pos_embed: float32 [196, 384], replicated, may hold values from -3 to 3
- mask_token: float32 [384], replicated, may hold values from -3 to 3
- enc_cot: bfloat16 [25088, 384], P('dp'), may hold values from -6 to 6
- reg_cot: bfloat16 [25088, 384], P('dp'), may hold values from -6 to 6
Outputs:
- encoded: bfloat16 [25088, 384], P('dp')
- predicted: bfloat16 [25088, 384], P('dp')
- input_grad: float32 [25088, 384], P('dp')
- grad_enc_qkv: float32 [3, 384, 384], P(None, None, 'tp')
- grad_enc_head_bias: float32 [2, 384], P(None, 'tp')
- grad_enc_proj: float32 [384, 384], P('tp')
- grad_enc_fc1: float32 [384, 1536], P(None, 'tp')
- grad_enc_fc1_bias: float32 [1536], P('tp')
- grad_enc_fc2: float32 [1536, 384], P('tp')
- grad_enc_gains: float32 [4, 384], replicated
- grad_enc_shifts: float32 [4, 384], replicated
- grad_reg_qkv: float32 [3, 384, 384], P(None, None, 'tp')
- grad_reg_head_bias: float32 [2, 384], P(None, 'tp')
- grad_reg_proj: float32 [384, 384], P('tp')
- grad_reg_fc1: float32 [384, 1536], P(None, 'tp')
- grad_reg_fc1_bias: float32 [1536], P('tp')
- grad_reg_fc2: float32 [1536, 384], P('tp')
- grad_reg_gains: float32 [5, 384], replicated
- grad_reg_shifts: float32 [5, 384], replicated
- grad_pos_embed: float32 [196, 384], replicated
- grad_mask_token: float32 [384], replicated
Inputs may be any that keep to these rules, and one draw needn't show every extreme that they name: `patch_order`: each row is a permutation of the 196 patch indices: the first 98 entries are the visible patches, the others the masked ones.
All inputs are finite; a program needn't handle non-finite values.
Results may differ from a plain program's by a relative error of at most 0.023.
Values may be sent and summed in bfloat16 or wider, within the bound.
No kernel may reach another device: no remote copies, remote signals or barrier semaphores. Data moves between devices by JAX's collectives and lax.ppermute only.
A program may use at most 192 MiB of HBM per device.

v0:
```python
from functools import partial

import jax
import jax.numpy as jnp
from jax import lax
from jax.sharding import PartitionSpec as P

HEAD_DIM = 64


epsilon = 1e-06


def norm_forward(values, gain_row, shift_row):
    centred = values - jnp.mean(values, axis=-1, keepdims=True)
    variance = jnp.mean(centred * centred, axis=-1, keepdims=True)
    row_scale = lax.rsqrt(variance + epsilon)
    unit_rows = centred * row_scale
    return (unit_rows * gain_row + shift_row, unit_rows, row_scale)


def norm_backward(grad_out, unit_rows, row_scale, gain_row):
    grad_unit = grad_out * gain_row
    grad_in = row_scale * (
        grad_unit
        - jnp.mean(grad_unit, axis=-1, keepdims=True)
        - unit_rows * jnp.mean(grad_unit * unit_rows, axis=-1, keepdims=True)
    )
    return (grad_in, jnp.sum(grad_out * unit_rows, axis=0), jnp.sum(grad_out, axis=0))


def matmul(left_side, right_side):
    return jnp.dot(left_side, right_side, preferred_element_type=jnp.float32)


def weight_grad(left_side, right_side):
    return lax.dot_general(
        left_side, right_side, (((0,), (0,)), ((), ())), preferred_element_type=jnp.float32
    )


def back_through(grad_rows, weight):
    return lax.dot_general(
        grad_rows, weight, (((1,), (1,)), ((), ())), preferred_element_type=jnp.float32
    )


def split_heads(rows, images):
    return rows.reshape(images, -1, rows.shape[1] // HEAD_DIM, HEAD_DIM)


def attend(queries, key_rows, value_rows, images):
    q_heads = split_heads(queries, images)
    k_heads = split_heads(key_rows, images)
    v_heads = split_heads(value_rows, images)
    scores = jnp.einsum(
        "bqhd,bkhd->bhqk", q_heads, k_heads, preferred_element_type=jnp.float32
    ) * HEAD_DIM ** (-0.5)
    row_max = jnp.max(scores, axis=-1, keepdims=True)
    weights = jnp.exp(scores - row_max)
    row_total = jnp.sum(weights, axis=-1, keepdims=True)
    chosen = (weights / row_total).astype(jnp.bfloat16)
    output = jnp.einsum("bhqk,bkhd->bqhd", chosen, v_heads, preferred_element_type=jnp.float32)
    return (output.reshape(queries.shape).astype(jnp.bfloat16), row_max + jnp.log(row_total))


def attend_back(queries, key_rows, value_rows, grad_mixed, log_total, images):
    q_heads = split_heads(queries, images)
    k_heads = split_heads(key_rows, images)
    v_heads = split_heads(value_rows, images)
    g_heads = split_heads(grad_mixed, images)
    scale_factor = HEAD_DIM ** (-0.5)
    scores = (
        jnp.einsum("bqhd,bkhd->bhqk", q_heads, k_heads, preferred_element_type=jnp.float32)
        * scale_factor
    )
    chances = jnp.exp(scores - log_total)
    grad_values = jnp.einsum(
        "bhqk,bqhd->bkhd", chances.astype(jnp.bfloat16), g_heads, preferred_element_type=jnp.float32
    )
    grad_chances = jnp.einsum(
        "bqhd,bkhd->bhqk", g_heads, v_heads, preferred_element_type=jnp.float32
    )
    grad_scores = (
        chances * (grad_chances - jnp.sum(grad_chances * chances, axis=-1, keepdims=True))
    ).astype(jnp.bfloat16)
    grad_queries = (
        jnp.einsum("bhqk,bkhd->bqhd", grad_scores, k_heads, preferred_element_type=jnp.float32)
        * scale_factor
    )
    grad_keys = (
        jnp.einsum("bhqk,bqhd->bkhd", grad_scores, q_heads, preferred_element_type=jnp.float32)
        * scale_factor
    )
    return (
        grad_queries.reshape(queries.shape).astype(jnp.bfloat16),
        grad_keys.reshape(key_rows.shape).astype(jnp.bfloat16),
        grad_values.reshape(value_rows.shape).astype(jnp.bfloat16),
    )


def mlp_forward(act_in, w_first, first_bias, w_second):
    before = matmul(act_in, w_first) + first_bias
    hidden = jax.nn.gelu(before, approximate=False).astype(jnp.bfloat16)
    return (before, hidden, matmul(hidden, w_second))


def mlp_backward(grad_low, act_in, before, hidden, w_first, w_second):
    grad_second = weight_grad(hidden, grad_low)
    grad_hidden = back_through(grad_low, w_second)
    grad_before = jax.vjp(partial(jax.nn.gelu, approximate=False), before)[1](grad_hidden)[
        0
    ].astype(jnp.bfloat16)
    return (
        back_through(grad_before, w_first),
        weight_grad(act_in, grad_before),
        jnp.sum(grad_before, axis=0, dtype=jnp.float32),
        grad_second,
    )


def branch_back(grad_state, branch, gain_row):
    grad_gain = jnp.sum(grad_state * branch, axis=0)
    grad_branch = grad_state * gain_row
    return (grad_branch.astype(jnp.bfloat16), grad_gain, jnp.sum(grad_branch, axis=0))


def body(
    x_visible,
    patch_order,
    enc_qkv,
    enc_head_bias,
    enc_proj,
    enc_fc1,
    enc_fc1_bias,
    enc_fc2,
    enc_gains,
    enc_shifts,
    reg_qkv,
    reg_head_bias,
    reg_proj,
    reg_fc1,
    reg_fc1_bias,
    reg_fc2,
    reg_gains,
    reg_shifts,
    pos_embed,
    mask_token,
    enc_cot,
    reg_cot,
):
    images = patch_order.shape[0]
    patches = patch_order.shape[1]
    seen_count = x_visible.shape[0] // images
    feat_width = x_visible.shape[1]
    inputs = x_visible.astype(jnp.float32)
    norm_one, unit_one, scale_one = norm_forward(inputs, enc_gains[0], enc_shifts[0])
    act_one = norm_one.astype(jnp.bfloat16)
    enc_query = (matmul(act_one, enc_qkv[0]) + enc_head_bias[0]).astype(jnp.bfloat16)
    enc_keys = matmul(act_one, enc_qkv[1]).astype(jnp.bfloat16)
    enc_values = (matmul(act_one, enc_qkv[2]) + enc_head_bias[1]).astype(jnp.bfloat16)
    enc_mixed, enc_logsum = attend(enc_query, enc_keys, enc_values, images)
    enc_attn = lax.psum(matmul(enc_mixed, enc_proj).astype(jnp.bfloat16), "tp").astype(jnp.float32)
    branch_one = enc_attn + enc_shifts[2]
    state_one = inputs + enc_gains[2] * branch_one
    norm_two, unit_two, scale_two = norm_forward(state_one, enc_gains[1], enc_shifts[1])
    act_two = norm_two.astype(jnp.bfloat16)
    before_two, hidden_two, enc_part = mlp_forward(act_two, enc_fc1, enc_fc1_bias, enc_fc2)
    enc_mlp = lax.psum(enc_part.astype(jnp.bfloat16), "tp").astype(jnp.float32)
    branch_two = enc_mlp + enc_shifts[3]
    encoded = state_one + enc_gains[3] * branch_two
    seen_index = patch_order[:, :seen_count].reshape(-1)
    masked_index = patch_order[:, seen_count:].reshape(-1)
    seen_pos = jnp.take(pos_embed, seen_index, axis=0)
    masked_pos = jnp.take(pos_embed, masked_index, axis=0)
    mask_rows = mask_token + masked_pos
    context = jnp.concatenate(
        [
            (encoded + seen_pos).reshape(images, seen_count, feat_width),
            mask_rows.reshape(images, -1, feat_width),
        ],
        axis=1,
    ).reshape(-1, feat_width)
    norm_three, unit_three, scale_three = norm_forward(mask_rows, reg_gains[0], reg_shifts[0])
    act_three = norm_three.astype(jnp.bfloat16)
    norm_four, unit_four, scale_four = norm_forward(context, reg_gains[1], reg_shifts[1])
    act_four = norm_four.astype(jnp.bfloat16)
    reg_query = (matmul(act_three, reg_qkv[0]) + reg_head_bias[0]).astype(jnp.bfloat16)
    reg_keys = matmul(act_four, reg_qkv[1]).astype(jnp.bfloat16)
    reg_values = (matmul(act_four, reg_qkv[2]) + reg_head_bias[1]).astype(jnp.bfloat16)
    reg_mixed, reg_logsum = attend(reg_query, reg_keys, reg_values, images)
    reg_attn = lax.psum(matmul(reg_mixed, reg_proj).astype(jnp.bfloat16), "tp").astype(jnp.float32)
    branch_three = reg_attn + reg_shifts[3]
    state_three = mask_rows + reg_gains[3] * branch_three
    norm_five, unit_five, scale_five = norm_forward(state_three, reg_gains[2], reg_shifts[2])
    act_five = norm_five.astype(jnp.bfloat16)
    before_five, hidden_five, reg_part = mlp_forward(act_five, reg_fc1, reg_fc1_bias, reg_fc2)
    reg_mlp = lax.psum(reg_part.astype(jnp.bfloat16), "tp").astype(jnp.float32)
    branch_four = reg_mlp + reg_shifts[4]
    predicted = state_three + reg_gains[4] * branch_four
    grad_pred = reg_cot.astype(jnp.float32)
    grad_low, grad_rgain4, grad_rshift4 = branch_back(grad_pred, branch_four, reg_gains[4])
    part_five, grad_reg_fc1, grad_reg_fc1_bias, grad_reg_fc2 = mlp_backward(
        grad_low, act_five, before_five, hidden_five, reg_fc1, reg_fc2
    )
    grad_act5 = lax.psum(part_five.astype(jnp.bfloat16), "tp").astype(jnp.float32)
    grad_in5, grad_rgain2, grad_rshift2 = norm_backward(
        grad_act5, unit_five, scale_five, reg_gains[2]
    )
    grad_state3 = grad_pred + grad_in5
    grad_low3, grad_rgain3, grad_rshift3 = branch_back(grad_state3, branch_three, reg_gains[3])
    grad_reg_proj = weight_grad(reg_mixed, grad_low3)
    grad_rmixed = back_through(grad_low3, reg_proj).astype(jnp.bfloat16)
    grad_rq, grad_rk, grad_rv = attend_back(
        reg_query, reg_keys, reg_values, grad_rmixed, reg_logsum, images
    )
    grad_reg_qkv = jnp.stack(
        [
            weight_grad(act_three, grad_rq),
            weight_grad(act_four, grad_rk),
            weight_grad(act_four, grad_rv),
        ]
    )
    grad_reg_head_bias = jnp.stack(
        [jnp.sum(grad_rq, axis=0, dtype=jnp.float32), jnp.sum(grad_rv, axis=0, dtype=jnp.float32)]
    )
    part_query = back_through(grad_rq, reg_qkv[0])
    part_context = back_through(grad_rk, reg_qkv[1]) + back_through(grad_rv, reg_qkv[2])
    grad_act3, grad_act4 = (
        lax.psum(part_query.astype(jnp.bfloat16), "tp").astype(jnp.float32),
        lax.psum(part_context.astype(jnp.bfloat16), "tp").astype(jnp.float32),
    )
    grad_in3, grad_rgain0, grad_rshift0 = norm_backward(
        grad_act3, unit_three, scale_three, reg_gains[0]
    )
    grad_context, grad_rgain1, grad_rshift1 = norm_backward(
        grad_act4, unit_four, scale_four, reg_gains[1]
    )
    grad_context = grad_context.reshape(images, patches, feat_width)
    grad_seen = grad_context[:, :seen_count].reshape(-1, feat_width)
    grad_masked = grad_state3 + grad_in3 + grad_context[:, seen_count:].reshape(-1, feat_width)
    grad_mask_token = jnp.sum(grad_masked, axis=0)
    grad_pos_embed = jax.ops.segment_sum(
        jnp.concatenate([grad_seen, grad_masked], axis=0),
        jnp.concatenate([seen_index, masked_index], axis=0),
        num_segments=patches,
    )
    grad_reg_gains = jnp.stack([grad_rgain0, grad_rgain1, grad_rgain2, grad_rgain3, grad_rgain4])
    grad_reg_shifts = jnp.stack(
        [grad_rshift0, grad_rshift1, grad_rshift2, grad_rshift3, grad_rshift4]
    )
    grad_enc = enc_cot.astype(jnp.float32) + grad_seen
    grad_low2, grad_egain3, grad_eshift3 = branch_back(grad_enc, branch_two, enc_gains[3])
    part_two, grad_enc_fc1, grad_enc_fc1_bias, grad_enc_fc2 = mlp_backward(
        grad_low2, act_two, before_two, hidden_two, enc_fc1, enc_fc2
    )
    grad_act2 = lax.psum(part_two.astype(jnp.bfloat16), "tp").astype(jnp.float32)
    grad_in2, grad_egain1, grad_eshift1 = norm_backward(
        grad_act2, unit_two, scale_two, enc_gains[1]
    )
    grad_state1 = grad_enc + grad_in2
    grad_low1, grad_egain2, grad_eshift2 = branch_back(grad_state1, branch_one, enc_gains[2])
    grad_enc_proj = weight_grad(enc_mixed, grad_low1)
    grad_emixed = back_through(grad_low1, enc_proj).astype(jnp.bfloat16)
    grad_eq, grad_ek, grad_ev = attend_back(
        enc_query, enc_keys, enc_values, grad_emixed, enc_logsum, images
    )
    grad_enc_qkv = jnp.stack(
        [
            weight_grad(act_one, grad_eq),
            weight_grad(act_one, grad_ek),
            weight_grad(act_one, grad_ev),
        ]
    )
    grad_enc_head_bias = jnp.stack(
        [jnp.sum(grad_eq, axis=0, dtype=jnp.float32), jnp.sum(grad_ev, axis=0, dtype=jnp.float32)]
    )
    part_one = (
        back_through(grad_eq, enc_qkv[0])
        + back_through(grad_ek, enc_qkv[1])
        + back_through(grad_ev, enc_qkv[2])
    )
    grad_act1 = lax.psum(part_one.astype(jnp.bfloat16), "tp").astype(jnp.float32)
    grad_in1, grad_egain0, grad_eshift0 = norm_backward(
        grad_act1, unit_one, scale_one, enc_gains[0]
    )
    input_grad = grad_state1 + grad_in1
    grad_enc_gains = jnp.stack([grad_egain0, grad_egain1, grad_egain2, grad_egain3])
    grad_enc_shifts = jnp.stack([grad_eshift0, grad_eshift1, grad_eshift2, grad_eshift3])
    (
        grad_enc_qkv,
        grad_enc_head_bias,
        grad_enc_proj,
        grad_enc_fc1,
        grad_enc_fc1_bias,
        grad_enc_fc2,
        grad_enc_gains,
        grad_enc_shifts,
        grad_reg_qkv,
        grad_reg_head_bias,
        grad_reg_proj,
        grad_reg_fc1,
        grad_reg_fc1_bias,
        grad_reg_fc2,
        grad_reg_gains,
        grad_reg_shifts,
        grad_pos_embed,
        grad_mask_token,
    ) = lax.psum(
        (
            grad_enc_qkv,
            grad_enc_head_bias,
            grad_enc_proj,
            grad_enc_fc1,
            grad_enc_fc1_bias,
            grad_enc_fc2,
            grad_enc_gains,
            grad_enc_shifts,
            grad_reg_qkv,
            grad_reg_head_bias,
            grad_reg_proj,
            grad_reg_fc1,
            grad_reg_fc1_bias,
            grad_reg_fc2,
            grad_reg_gains,
            grad_reg_shifts,
            grad_pos_embed,
            grad_mask_token,
        ),
        "dp",
    )
    return (
        encoded.astype(jnp.bfloat16),
        predicted.astype(jnp.bfloat16),
        input_grad,
        grad_enc_qkv,
        grad_enc_head_bias,
        grad_enc_proj,
        grad_enc_fc1,
        grad_enc_fc1_bias,
        grad_enc_fc2,
        grad_enc_gains,
        grad_enc_shifts,
        grad_reg_qkv,
        grad_reg_head_bias,
        grad_reg_proj,
        grad_reg_fc1,
        grad_reg_fc1_bias,
        grad_reg_fc2,
        grad_reg_gains,
        grad_reg_shifts,
        grad_pos_embed,
        grad_mask_token,
    )


def solution(mesh):
    placed = (
        P("dp", None),
        P("dp", None),
        P(None, None, "tp"),
        P(None, "tp"),
        P("tp", None),
        P(None, "tp"),
        P("tp"),
        P("tp", None),
        P(),
        P(),
        P(None, None, "tp"),
        P(None, "tp"),
        P("tp", None),
        P(None, "tp"),
        P("tp"),
        P("tp", None),
        P(),
        P(),
        P(),
        P(),
        P("dp", None),
        P("dp", None),
    )
    return jax.shard_map(
        body,
        mesh=mesh,
        in_specs=placed,
        out_specs=(
            P("dp", None),
            P("dp", None),
            P("dp", None),
            P(None, None, "tp"),
            P(None, "tp"),
            P("tp", None),
            P(None, "tp"),
            P("tp"),
            P("tp", None),
            P(),
            P(),
            P(None, None, "tp"),
            P(None, "tp"),
            P("tp", None),
            P(None, "tp"),
            P("tp"),
            P("tp", None),
            P(),
            P(),
            P(),
            P(),
        ),
        check_vma=False,
    )
```

profile of v0, /device:TPU:0, one launch (start us, length us, event | category | flops | bytes accessed | tf_op | source)
XLA Modules:
  0.0 722.3 jit_solution(9807891342569373064)
XLA Ops:
  15.3 3.4 reshape.622
  20.2 3.5 reshape.621
  23.8 2.8 reshape.623
  30.8 2.7 convolution_convert_fusion.3
  34.4 5.3 gather_fusion.1
  39.9 5.4 gather_fusion
  45.9 10.3 %all-reduce.12.cloned.1.call-done = bf16[1568,384]{1,0:T(8,128)(2,1)} async-done(((bf16[1568,384]{1,0:T(8,128)(2,1)}), bf16[1568,384]{1,0:T(8,128)(2,1)}) %all-reduce.12.cloned.1.call-update) | async-done | bytes 1204240 | tf_op jit(solution)/shard_map/psum | solution.py:163
  56.3 4.1 fusion.169
  61.4 2.9 reshape.627
  64.3 14.5 %multiply_convert_fusion.2 = (bf16[1568,768]{1,0:T(8,128)(2,1)S(1)}, f32[1568,768]{1,0:T(8,128)}, f32[1568,768]{1,0:T(8,128)}) fusion(f32[768]{0:T(1024)S(1)} %copy-done.139, bf16[384,768]{1,0:T(8,128)(2,1)} %param.29, f32[384]{0:T(512)S(1)} %get-tuple-element.67, f32[384]{0:T(512)S(1)} %get-tuple-element.63, f32[1568]{0:T(1024)S(1)} %add_rsqrt_fusion.3, ...), kind=kOutput, calls=%fused_computation.52 | convolution fusion | flops 1010343936 | bytes 15062272 | tf_op jit(solution)/shard_map/dot_general | solution.py:33
  88.4 3.4 reshape.629
  91.8 12.1 %all-reduce.14.cloned.1.call-done = bf16[1568,384]{1,0:T(8,128)(2,1)} async-done(((bf16[1568,384]{1,0:T(8,128)(2,1)}), bf16[1568,384]{1,0:T(8,128)(2,1)}) %all-reduce.14.cloned.1.call-update) | async-done | bytes 1204240 | tf_op jit(solution)/shard_map/psum | solution.py:169
  103.9 4.1 select_add_fusion
  108.0 2.9 reshape.626
  110.9 3.1 fusion.170
  118.3 4.0 convert_element_type.296
  122.4 4.0 convolution_convert_fusion
  128.4 6.7 reshape.628
  135.1 6.9 reshape.630
  142.0 3.7 multiply_reduce_fusion.2
  154.1 2.7 convolution_convert_fusion.2
  156.9 21.2 %all-reduce.16.cloned.1.call-done = bf16[1568,384]{1,0:T(8,128)(2,1)} async-done(((bf16[1568,384]{1,0:T(8,128)(2,1)}), bf16[1568,384]{1,0:T(8,128)(2,1)}) %all-reduce.16.cloned.1.call-update) | async-done | bytes 1204240 | tf_op jit(solution)/shard_map/psum | solution.py:192
  181.4 13.1 %multiply_convert_fusion.1 = (bf16[1568,768]{1,0:T(8,128)(2,1)}, f32[1568,768]{1,0:T(8,128)S(1)}, f32[1568,768]{1,0:T(8,128)S(1)}) fusion(f32[768]{0:T(1024)S(1)} %copy-done.138, bf16[384,768]{1,0:T(8,128)(2,1)S(1)} %copy-done, f32[1568,384]{1,0:T(8,128)S(1)} %get-tuple-element.96, f32[384]{0:T(512)S(1)} %copy-done.102, f32[384]{0:T(512)S(1)} %copy-done.97, ...), kind=kOutput, calls=%fused_computation.39 | convolution fusion | flops 1007333376 | bytes 15059200 | tf_op jit(solution)/shard_map/dot_general | solution.py:33
  194.5 3.6 convert_reduce_fusion.1
  202.9 20.4 %all-reduce.18.cloned.1.call-done = bf16[1568,384]{1,0:T(8,128)(2,1)} async-done(((bf16[1568,384]{1,0:T(8,128)(2,1)}), bf16[1568,384]{1,0:T(8,128)(2,1)}) %all-reduce.18.cloned.1.call-update) | async-done | bytes 1204240 | tf_op jit(solution)/shard_map/psum | solution.py:206
  223.3 4.0 fusion.74
  227.3 4.5 multiply_reduce_fusion.12
  234.6 3.4 reshape.631
  238.1 5.1 convert_reduce_fusion.8
  243.2 7.0 multiply_reduce_fusion
  252.2 4.3 convert_element_type.327
  256.5 5.3 multiply_convert_fusion
  266.9 4.4 convert_element_type.323
  278.7 5.2 reshape.632
  283.9 15.5 %all-reduce.20.cloned.1.call-done = bf16[3136,384]{1,0:T(8,128)(2,1)} async-done(((bf16[3136,384]{1,0:T(8,128)(2,1)}), bf16[3136,384]{1,0:T(8,128)(2,1)}) %all-reduce.20.cloned.1.call-update) | async-done | bytes 2408464 | tf_op jit(solution)/shard_map/psum | solution.py:231
  299.4 5.6 fusion.10
  305.1 4.4 fusion.6
  309.4 5.1 reshape.633
  314.6 5.0 fusion.172
  319.6 2.9 reshape.634
  322.5 8.0 %convert_reduce_fusion.2 = (f32[768]{0:T(1024)S(1)}, bf16[1568,768]{1,0:T(8,128)(2,1)S(1)}) fusion(f32[1568,768]{1,0:T(8,128)} %get-tuple-element.102, bf16[768,384]{1,0:T(8,128)(2,1)} %param.31, f32[384]{0:T(512)S(1)} %copy-done.114, f32[1568,384]{1,0:T(8,128)} %reshape.634, bf16[1568,384]{1,0:T(8,128)(2,1)} %param.44, ...), kind=kOutput, calls=%fused_computation.35 | convolution fusion | flops 947723520 | bytes 16252416 | tf_op jit(solution)/shard_map/dot_general | solution.py:43
  334.8 4.4 convolution_convert_fusion.6
  339.2 2.6 fusion.160
  344.7 2.6 convert_element_type.354
  347.3 2.7 convolution_convert_fusion.1
  350.0 5.6 all-reduce.22.cloned.1.call-done
  355.7 3.0 fusion.75
  358.8 4.1 multiply_reduce_fusion.11
  365.8 3.4 reshape.635
  369.3 3.2 convert_reduce_fusion.10
  379.5 2.6 convert_element_type.346
  384.7 3.0 convert_element_type.342
  390.3 2.6 convert_element_type.339
  398.2 4.8 fusion.108
  408.4 3.2 reshape.636
  411.6 5.5 fusion.126
  417.1 2.7 fusion.162
  424.9 3.4 fusion.64
  428.4 4.0 fusion.164
  432.4 23.8 %scatter_custom_fusion = f32[196,384]{1,0:T(8,128)} fusion(s32[3136]{0:T(1024)} %pad_add_fusion, f32[1568,384]{1,0:T(8,128)} %get-tuple-element.90, f32[]{:T(128)} %constant.47.clone.1, f32[1568,384]{1,0:T(8,128)} %reshape.634, f32[]{:T(128)} %constant.43.clone.1), kind=kCustom, calls=%fused_computation.30 | custom fusion | flops 2408448 | bytes 5118976 | tf_op jit(solution)/shard_map/scatter-add | solution.py:243
  457.6 3.9 fusion.43
  463.2 81.4 %all-reduce = (f32[2,192]{1,0:T(2,128)}, f32[768]{0:T(1024)}, f32[4,384]{1,0:T(4,128)}, f32[4,384]{1,0:T(4,128)}, f32[2,192]{1,0:T(2,128)}, /*index=5*/f32[768]{...) all-reduce(f32[2,192]{1,0:T(2,128)S(1)} %pad_maximum_fusion.5, ...), channel_id=1, replica_groups=mesh['dp'=16,'tp'=2] {'dp'}, use_global_device_ids=true, to_apply=%region_35.37 | all-reduce | flops 9600 | bytes 76800 | tf_op jit(solution)/shard_map/psum | solution.py:309
  544.6 3.5 fusion.58
  548.1 156.8 %all-reduce.24.cloned.1.call-done = (f32[3,384,192]{1,2,0:T(8,128)}, f32[192,384]{1,0:T(8,128)}, f32[384,768]{1,0:T(8,128)}, f32[768,384]{1,0:T(8,128)}, f32[3,3...) async-done(((f32[3,384,192]{1,2,0:T(8,128)}, f32[192,384]{1,0:T(8,128)}, f32[384,768]{1,0:T(8,128)}, ...) | async-done | bytes 7378960 | tf_op jit(solution)/shard_map/psum | solution.py:309
  (438 shorter events, 116.5 us)
Async XLA Ops:
  7.2 174.0 %copy-start = (bf16[384,768]{1,0:T(8,128)(2,1)S(1)}, bf16[384,768]{1,0:T(8,128)(2,1)}, u32[]{:S(2)}) copy-start(bf16[384,768]{1,0:T(8,128)(2,1)} %param.37) | copy-start | bytes 1769476
  7.2 4.7 copy-start.3
  7.2 4.5 copy-start.126
  7.2 4.5 copy-start.127
  7.2 49.0 %all-reduce.12.cloned.1.call-start = ((), (), s32[]{:S(2)}) async-start(), calls=%async_computation | async-start | bytes 2408448 | tf_op jit(solution)/shard_map/psum | solution.py:163
  11.8 52.5 %copy-start.111 = (f32[384]{0:T(512)}, f32[384]{0:T(512)S(1)}, u32[]{:S(2)}) copy-start(f32[384]{0:T(512)S(1)} %get-tuple-element.63) | copy-start | bytes 4612
  11.8 92.1 %copy-start.87 = (f32[384]{0:T(512)}, f32[384]{0:T(512)S(1)}, u32[]{:S(2)}) copy-start(f32[384]{0:T(512)S(1)} %get-tuple-element.62) | copy-start | bytes 4612
  11.8 92.1 %copy-start.113 = (f32[384]{0:T(512)}, f32[384]{0:T(512)S(1)}, u32[]{:S(2)}) copy-start(f32[384]{0:T(512)S(1)} %get-tuple-element.60) | copy-start | bytes 4612
  11.8 52.5 %copy-start.132 = (f32[384]{0:T(512)}, f32[384]{0:T(512)S(1)}, u32[]{:S(2)}) copy-start(f32[384]{0:T(512)S(1)} %get-tuple-element.67) | copy-start | bytes 4612
  11.8 92.1 %copy-start.93 = (f32[384]{0:T(512)}, f32[384]{0:T(512)S(1)}, u32[]{:S(2)}) copy-start(f32[384]{0:T(512)S(1)} %get-tuple-element.65) | copy-start | bytes 4612
  11.8 92.1 %copy-start.115 = (f32[384]{0:T(512)}, f32[384]{0:T(512)S(1)}, u32[]{:S(2)}) copy-start(f32[384]{0:T(512)S(1)} %get-tuple-element.64) | copy-start | bytes 4612
  12.4 6.4 copy-start.18
  20.2 6.3 copy-start.30
  29.8 4.7 copy-start.1
  30.8 9.0 %copy-start.37 = (bf16[1568,192]{0,1:T(8,128)(2,1)}, bf16[1568,192]{0,1:T(8,128)(2,1)S(1)}, u32[]{:S(2)}) copy-start(bf16[1568,192]{0,1:T(8,128)(2,1)S(1)} %convert_element_type.287) | copy-start | bytes 1806340
  33.6 70.3 %all-reduce.14.cloned.1.call-start = ((), (), s32[]{:S(2)}) async-start(), calls=%async_computation.1 | async-start | bytes 2408448 | tf_op jit(solution)/shard_map/psum | solution.py:169
  34.3 11.6 %copy-start.83 = (s32[1568]{0:T(1024)}, s32[1568]{0:T(1024)S(1)}, u32[]{:S(2)}) copy-start(s32[1568]{0:T(1024)S(1)} %reshape.625) | copy-start | bytes 18820
  34.4 11.5 %copy-start.85 = (s32[1568]{0:T(1024)}, s32[1568]{0:T(1024)S(1)}, u32[]{:S(2)}) copy-start(s32[1568]{0:T(1024)S(1)} %reshape.624) | copy-start | bytes 18820
  39.8 5.4 copy-start.128
  39.8 5.4 copy-start.129
  39.8 6.0 copy-start.134
  39.8 16.4 %copy-start.131 = (f32[384]{0:T(512)S(1)}, f32[384]{0:T(512)}, u32[]{:S(2)}) copy-start(f32[384]{0:T(512)} %param.43) | copy-start | bytes 4612
  45.9 39.5 %copy-start.104 = (f32[384]{0:T(512)}, f32[384]{0:T(512)S(1)}, u32[]{:S(2)}) copy-start(f32[384]{0:T(512)S(1)} %get-tuple-element.143) | copy-start | bytes 4612
  45.9 69.5 %copy-start.106 = (f32[384]{0:T(512)}, f32[384]{0:T(512)S(1)}, u32[]{:S(2)}) copy-start(f32[384]{0:T(512)S(1)} %get-tuple-element.142) | copy-start | bytes 4612
  45.9 132.2 %copy-start.99 = (f32[384]{0:T(512)}, f32[384]{0:T(512)S(1)}, u32[]{:S(2)}) copy-start(f32[384]{0:T(512)S(1)} %get-tuple-element.141) | copy-start | bytes 4612
  45.9 132.2 %copy-start.110 = (f32[384]{0:T(512)}, f32[384]{0:T(512)S(1)}, u32[]{:S(2)}) copy-start(f32[384]{0:T(512)S(1)} %get-tuple-element.56) | copy-start | bytes 4612
  60.4 24.9 %copy-start.77 = (f32[1568]{0:T(1024)}, f32[1568]{0:T(1024)S(1)}, u32[]{:S(2)}) copy-start(f32[1568]{0:T(1024)S(1)} %broadcast_multiply_fusion.12) | copy-start | bytes 18820
  64.3 15.9 %copy-start.135 = (bf16[768,384]{1,0:T(8,128)(2,1)S(1)}, bf16[768,384]{1,0:T(8,128)(2,1)}, u32[]{:S(2)}) copy-start(bf16[768,384]{1,0:T(8,128)(2,1)} %param.31) | copy-start | bytes 1769476
  82.7 95.4 %all-reduce.16.cloned.1.call-start = ((), (), s32[]{:S(2)}) async-start(), calls=%async_computation.2 | async-start | bytes 2408448 | tf_op jit(solution)/shard_map/psum | solution.py:192
  156.8 66.4 %all-reduce.18.cloned.1.call-start = ((), (), s32[]{:S(2)}) async-start(), calls=%async_computation.3 | async-start | bytes 2408448 | tf_op jit(solution)/shard_map/psum | solution.py:206
  180.5 13.9 %copy-start.6 = (f32[1568,384]{1,0:T(8,128)}, f32[1568,384]{1,0:T(8,128)S(1)}, u32[]{:S(2)}) copy-start(f32[1568,384]{1,0:T(8,128)S(1)} %get-tuple-element.96) | copy-start | bytes 7225348
  181.4 13.1 %copy-start.50 = (bf16[1568,384]{1,0:T(8,128)(2,1)S(1)}, bf16[1568,384]{1,0:T(8,128)(2,1)}, u32[]{:S(2)}) copy-start(bf16[1568,384]{1,0:T(8,128)(2,1)} %param.45) | copy-start | bytes 3612676
  181.4 13.1 %copy-start.119 = (f32[384]{0:T(512)S(1)}, f32[384]{0:T(512)}, u32[]{:S(2)}) copy-start(f32[384]{0:T(512)} %get-tuple-element.144) | copy-start | bytes 4612
  181.4 13.1 %copy-start.137 = (bf16[768,384]{1,0:T(8,128)(2,1)S(1)}, bf16[768,384]{1,0:T(8,128)(2,1)}, u32[]{:S(2)}) copy-start(bf16[768,384]{1,0:T(8,128)(2,1)} %param.39) | copy-start | bytes 1769476
  202.1 97.3 %all-reduce.20.cloned.1.call-start = ((), (), s32[]{:S(2)}) async-start(), calls=%async_computation.4 | async-start | bytes 4816896 | tf_op jit(solution)/shard_map/psum | solution.py:231
  227.3 5.9 copy-start.69
  227.3 5.9 copy-start.100
  238.1 5.1 copy-start.28
  238.1 5.1 copy-start.36
  256.5 6.7 copy-start.27
  276.4 79.3 %all-reduce.22.cloned.1.call-start = ((), (), s32[]{:S(2)}) async-start(), calls=%async_computation.5 | async-start | bytes 2408448 | tf_op jit(solution)/shard_map/psum | solution.py:257
  278.7 20.7 %copy-start.107 = (f32[384]{0:T(512)S(1)}, f32[384]{0:T(512)}, u32[]{:S(2)}) copy-start(f32[384]{0:T(512)} %copy-done.106) | copy-start | bytes 4612
  299.4 5.6 copy-start.12
  299.4 5.7 copy-start.25
  322.5 9.4 %copy-start.136 = (bf16[384,768]{1,0:T(8,128)(2,1)S(1)}, bf16[384,768]{1,0:T(8,128)(2,1)}, u32[]{:S(2)}) copy-start(bf16[384,768]{1,0:T(8,128)(2,1)} %param.29) | copy-start | bytes 1769476
  334.5 90.4 %all-reduce.26.cloned.1.call-start = ((), (), s32[]{:S(2)}) async-start(), calls=%async_computation.7 | async-start | bytes 7225344 | tf_op jit(solution)/shard_map/psum | solution.py:198
  334.7 4.4 copy-start.8
  343.2 12.4 %copy-start.80 = (f32[1568]{0:T(1024)S(1)}, f32[1568]{0:T(1024)}, u32[]{:S(2)}) copy-start(f32[1568]{0:T(1024)} %copy-done.79) | copy-start | bytes 18820
  343.2 12.4 %copy-start.88 = (f32[384]{0:T(512)S(1)}, f32[384]{0:T(512)}, u32[]{:S(2)}) copy-start(f32[384]{0:T(512)} %copy-done.87) | copy-start | bytes 4612
  343.2 12.4 %copy-start.94 = (f32[384]{0:T(512)S(1)}, f32[384]{0:T(512)}, u32[]{:S(2)}) copy-start(f32[384]{0:T(512)} %copy-done.93) | copy-start | bytes 4612
  343.2 12.4 %copy-start.96 = (f32[1568]{0:T(1024)S(1)}, f32[1568]{0:T(1024)}, u32[]{:S(2)}) copy-start(f32[1568]{0:T(1024)} %copy-done.95) | copy-start | bytes 18820
  343.3 12.4 %copy-start.112 = (f32[384]{0:T(512)S(1)}, f32[384]{0:T(512)}, u32[]{:S(2)}) copy-start(f32[384]{0:T(512)} %copy-done.111) | copy-start | bytes 4612
  347.3 11.5 %copy-start.116 = (f32[384]{0:T(512)S(1)}, f32[384]{0:T(512)}, u32[]{:S(2)}) copy-start(f32[384]{0:T(512)} %copy-done.115) | copy-start | bytes 4612
  358.8 5.6 copy-start.70
  384.7 8.2 %copy-start.67 = (bf16[3,384,192]{1,2,0:T(8,128)(2,1)S(1)}, bf16[3,384,192]{1,2,0:T(8,128)(2,1)}, u32[]{:S(2)}) copy-start(bf16[3,384,192]{1,2,0:T(8,128)(2,1)} %param.26) | copy-start | bytes 1327108
  397.5 307.3 %all-reduce.24.cloned.1.call-start = ((), (), s32[]{:S(2)}) async-start(), calls=%async_computation.6 | async-start | bytes 14770176 | tf_op jit(solution)/shard_map/psum | solution.py:309
  398.2 4.8 copy-start.41
  398.2 4.8 copy-start.53
  398.2 5.3 copy-start.22
  398.2 5.3 copy-start.47
  411.6 5.5 copy-start.133
  411.6 5.5 copy-start.143
  461.6 83.0 %copy-start.55 = (bf16[1568,384]{1,0:T(8,128)(2,1)S(1)}, bf16[1568,384]{1,0:T(8,128)(2,1)}, u32[]{:S(2)}) copy-start(bf16[1568,384]{1,0:T(8,128)(2,1)} %get-tuple-element.87) | copy-start | bytes 3612676
  704.9 5.0 copy-start.63
  (88 other events, 207.7 us)
Sparse Core Ops, SparseCore 0:
  33.7 22.5 all-reduce.11
  82.8 21.0 all-reduce.13
  157.0 21.0 all-reduce.15
  202.2 21.0 all-reduce.17
  276.5 22.8 all-reduce.19
  334.6 21.0 all-reduce.21
  397.6 25.4 all-reduce.25
  456.5 248.3 all-reduce.23
where the time goes:
time: 732 us; the launch traced here: 722 us
  waiting for transfers between devices  242 us (33%)
  local copies, waits for them, and re-layouts  143 us (20%)
  matrix products  135 us (18%)
  other arithmetic  104 us (14%)
  blocking collectives  81.4 us (11%)
  between operations  16 us (2%)
    psum x1, waiting for transfers between devices, body(): lax.psum((grad_enc_qkv, grad_enc_head_bias, grad_enc_proj, grad_enc_fc1,...  157 us
    psum x1, blocking collectives, body(): lax.psum((grad_enc_qkv, grad_enc_head_bias, grad_enc_proj, grad_enc_fc1,...  81.4 us
    dot_general x12, matrix products, matmul(): return jnp.dot(left_side, right_side, preferred_element_type=jnp.float32)  51.7 us
    reshape x8, local copies, waits for them, and re-layouts, split_heads(): return rows.reshape(images, -1, rows.shape[1] // HEAD_DIM, HEAD_DIM)  33.6 us
    dot_general x12, matrix products, back_through(): lax.dot_general(grad_rows, weight, (((1,), (1,)), ((), ())), preferred_el...  31.3 us
    unnamed x297, local copies, waits for them, and re-layouts  28.3 us
    scatter-add x1, other arithmetic, body(): jax.ops.segment_sum(jnp.concatenate([grad_seen, grad_masked], axis=0), jn...  23.8 us
    dot_general x12, matrix products, weight_grad(): lax.dot_general(left_side, right_side, (((0,), (0,)), ((), ())), preferre...  21.6 us
  transfers between devices with their start and end apart: 8, of which 7 were waited for; matrix products, arithmetic and copies ran while one was open for 10% of the time, Pallas kernels for 0%

commit v1 on v0

v1 whole, which is shorter than its diff:
```python
import functools

import jax
import jax.numpy as jnp
from jax import lax
from jax.experimental import pallas as pl
from jax.experimental.pallas import tpu as pltpu
from jax.sharding import PartitionSpec as P

HEAD_DIM = 64
EPSILON = 1e-06
F32 = jnp.float32
BF16 = jnp.bfloat16
LANES = 128
STEP = 96
QUERY = 112
KEYS = 128
CHUNK = 112
VMEM_LIMIT = 56 << 20


def dot(a, b, ca=1, cb=0):
    return lax.dot_general(a, b, (((ca,), (cb,)), ((), ())), preferred_element_type=F32)


def mean_row(v):
    return jnp.mean(v, axis=-1, keepdims=True)


def unit_rows(v):
    centred = v - mean_row(v)
    scale = lax.rsqrt(mean_row(centred * centred) + EPSILON)
    return centred * scale, scale


def norm_back(grad, unit, scale, gain):
    grad_unit = grad * gain
    return scale * (grad_unit - mean_row(grad_unit) - unit * mean_row(grad_unit * unit))


def fold(v):
    return jnp.sum(v.reshape(v.shape[0] // 8, 8, v.shape[1]), axis=0)


def total(v):
    return jnp.sum(v, axis=0, keepdims=True)


def gelu_pair(f):
    bell = jnp.exp(f * f * -0.5)
    t = 1.0 / (1.0 + 0.23164188 * jnp.abs(f))
    poly = t * (0.127414796 + t * (-0.142248368 + t * (0.7107068705 + t * (-0.7265760135 + t * 0.5307027145))))
    tail = poly * bell
    cdf = jnp.where(f >= 0.0, 1.0 - tail, tail)
    return f * cdf, cdf + f * bell * 0.3989422804014327


def rows_loop(rows, step):
    def go(c, carry):
        step(pl.ds(pl.multiple_of(c * CHUNK, 16), CHUNK))
        return carry

    lax.fori_loop(0, rows // CHUNK, go, 0)


def transposed(dst, src, rows):
    width = src.shape[1]
    dst[0:width, :] = src[0:rows, :].T
    dst[width:, :] = jnp.ones((16, rows), BF16)


def window(i):
    return pl.multiple_of(i * STEP, 32)


def head_masks():
    lane = lax.broadcasted_iota(jnp.int32, (KEYS, LANES), 1)
    return lane < HEAD_DIM


def split_pair(v, low):
    zero = jnp.zeros_like(v)
    return jnp.where(low, v, zero), jnp.where(low, zero, v)


def softmax_blocks(scores, i, vis, per_head):
    rows, width = scores.shape
    lane = lax.broadcasted_iota(jnp.int32, (rows, LANES), 1)
    row = lax.broadcasted_iota(jnp.int32, (rows, LANES), 0)
    low = 2 * i
    keys = (lane >= low) & (lane < low + vis)
    queries = (row >= low) & (row < low + vis)
    outs = []
    for h in range(2):
        blocks = []
        for b in range(per_head):
            at = (h * per_head + b) * LANES
            blocks.append(jnp.where(keys, scores[:, at : at + LANES], -1e30))
        top = functools.reduce(jnp.maximum, blocks)
        top = jnp.max(top, axis=-1, keepdims=True)
        blocks = [jnp.exp(b - top) for b in blocks]
        weight = 1.0 / jnp.sum(functools.reduce(jnp.add, blocks), axis=-1, keepdims=True)
        outs += [jnp.where(queries, b * weight, 0.0).astype(BF16) for b in blocks]
    return jnp.concatenate(outs, axis=1)


def put_window(ref, start, lanes, value):
    head = pl.ds(start, 16)
    ref[head, lanes] = ref[head, lanes] + value[:16]
    ref[pl.ds(start + 16, QUERY - 16), lanes] = value[16:QUERY]


def attend_back(chance, grad_out, value_stack, per_head):
    grad_chance = dot(grad_out, value_stack, 1, 1)
    p = chance.astype(F32)
    weighted = p * grad_chance
    outs = []
    for h in range(2):
        at = h * per_head * LANES
        parts = [weighted[:, at + b * LANES : at + (b + 1) * LANES] for b in range(per_head)]
        row = jnp.sum(functools.reduce(jnp.add, parts), axis=-1, keepdims=True)
        outs += [
            parts[b] - p[:, at + b * LANES : at + (b + 1) * LANES] * row for b in range(per_head)
        ]
    return jnp.concatenate(outs, axis=1).astype(BF16)


def join_columns(dst, own, other, count):
    half = own.shape[-1]
    for k in range(count):
        dst[:, 2 * half * k : 2 * half * (k + 1)] = jnp.concatenate([own[k], other[k]], axis=-1)


def head_bias_row(own, other):
    q = jnp.concatenate([own[0:1, :], other[0:1, :]], axis=-1)
    v = jnp.concatenate([own[1:2, :], other[1:2, :]], axis=-1)
    return q, v


def enc_attn_kernel(
    vis, tp, x_hbm, own_qkv, oth_qkv, own_proj, oth_proj, own_bias, oth_bias, gains, shifts,
    x1, act_t, qkv, chance, mixed, branch, weight,
    x_s, act_s, u_s, sem,
):
    rows, width = x1.shape
    images = rows // vis
    start = pl.multiple_of(tp[0] * rows, 16)
    copy = pltpu.make_async_copy(x_hbm.at[pl.ds(start, rows), :], x_s, sem)
    copy.start()
    join_columns(weight, own_qkv, oth_qkv, 3)
    copy.wait()

    def norm(at):
        unit, _ = unit_rows(x_s[at, :].astype(F32))
        act_s[at, :] = (unit * gains[0:1, :] + shifts[0:1, :]).astype(BF16)

    rows_loop(rows, norm)
    transposed(act_t, act_s, rows)
    bias_q, bias_v = head_bias_row(own_bias, oth_bias)
    qkv[rows:, :] = jnp.zeros((16, 3 * width), BF16)
    act = act_s[...]
    qkv[0:rows, 0:width] = ((dot(act, weight[:, 0:width]) + bias_q) * HEAD_DIM**-0.5).astype(BF16)
    qkv[0:rows, width : 2 * width] = dot(act, weight[:, width : 2 * width]).astype(BF16)
    qkv[0:rows, 2 * width :] = (dot(act, weight[:, 2 * width :]) + bias_v).astype(BF16)
    mixed[0:16, :] = jnp.zeros((16, width), BF16)
    low = head_masks()
    pairs = width // LANES

    def image(i, carry):
        at = window(i)
        for p in range(pairs):
            lanes = slice(p * LANES, (p + 1) * LANES)
            q = qkv[pl.ds(at, QUERY), lanes]
            k = qkv[pl.ds(at, KEYS), width + p * LANES : width + (p + 1) * LANES]
            v = qkv[pl.ds(at, KEYS), 2 * width + p * LANES : 2 * width + (p + 1) * LANES]
            scores = dot(q, jnp.concatenate(split_pair(k, low), axis=0), 1, 1)
            chosen = softmax_blocks(scores, i, vis, 1)
            chance[i * pairs + p] = chosen
            out = dot(chosen, jnp.concatenate(split_pair(v, low), axis=0)).astype(BF16)
            put_window(mixed, at, lanes, out)
        return carry

    lax.fori_loop(0, images, image, 0)
    half = own_proj.shape[0]
    u_s[...] = dot(mixed[:, 0:half], own_proj[...]) + dot(mixed[:, half:], oth_proj[...])

    def finish(at):
        u = u_s[at, :]
        branch[at, :] = u.astype(BF16)
        x1[at, :] = x_s[at, :].astype(F32) + gains[2:3, :] * (u + shifts[2:3, :])

    rows_loop(rows, finish)


def feed_forward(act_s, own_fc1, oth_fc1, own_b1, oth_b1, own_fc2, oth_fc2, hid, slope):
    half = own_fc1.shape[1]
    piece = 256

    def go(j, carry):
        at = pl.multiple_of(j * piece, piece)
        for w, b, base in ((own_fc1, own_b1, 0), (oth_fc1, oth_b1, half)):
            f = dot(act_s[...], w[:, pl.ds(at, piece)]) + b[:, pl.ds(at, piece)]
            h, g = gelu_pair(f)
            to = pl.ds(pl.multiple_of(base + at, piece), piece)
            hid[:, to] = h.astype(BF16)
            slope[:, to] = g.astype(BF16)
        return carry

    lax.fori_loop(0, half // piece, go, 0)
    return dot(hid[:, 0:half], own_fc2[...]) + dot(hid[:, half:], oth_fc2[...])


def feed_forward_back(
    d_low, act_t, own_fc1, oth_fc1, own_fc2, oth_fc2, hid, slope, d_before, own_out, oth_out, bias
):
    width, half = own_fc1.shape
    piece = 256
    for side, (w2, out) in enumerate(((own_fc2, own_out), (oth_fc2, oth_out))):
        base = side * half

        def go(j, carry, w2=w2, out=out, base=base):
            at = pl.multiple_of(j * piece, piece)
            cols = pl.ds(pl.multiple_of(base + at, piece), piece)
            grad_hid = dot(d_low[...], w2[pl.ds(at, piece), :], 1, 1)
            d_before[:, cols] = (grad_hid * slope[:, cols].astype(F32)).astype(BF16)
            out[pl.ds(pl.multiple_of(half + at, piece), piece), :] = dot(
                hid[:, cols], d_low[...], 0, 0
            ).astype(BF16)
            return carry

        lax.fori_loop(0, half // piece, go, 0)
        for c in range(half // width):
            cols = slice(base + c * width, base + (c + 1) * width)
            g = dot(act_t[...], d_before[:, cols])
            out[c * width : (c + 1) * width, :] = g[:width].astype(BF16)
            bias(side * (half // width) + c, g[width : width + 1])
    return dot(d_before[:, 0:half], own_fc1[...], 1, 1) + dot(d_before[:, half:], oth_fc1[...], 1, 1)


def enc_ffn_kernel(
    x1, own_fc1, oth_fc1, own_b1, oth_b1, own_fc2, oth_fc2, gains, shifts,
    state, encoded, act_t, hid, slope, branch,
    act_s, u_s,
):
    rows, width = x1.shape

    def norm(at):
        unit, _ = unit_rows(x1[at, :])
        act_s[at, :] = (unit * gains[1:2, :] + shifts[1:2, :]).astype(BF16)

    rows_loop(rows, norm)
    transposed(act_t, act_s, rows)
    u_s[...] = feed_forward(act_s, own_fc1, oth_fc1, own_b1, oth_b1, own_fc2, oth_fc2, hid, slope)

    def finish(at):
        u = u_s[at, :]
        branch[at, :] = u.astype(BF16)
        e = x1[at, :] + gains[3:4, :] * (u + shifts[3:4, :])
        state[at, :] = e
        encoded[at, :] = e.astype(BF16)

    rows_loop(rows, finish)


def one_hot(index, patches):
    lane = lax.broadcasted_iota(jnp.int32, (index.shape[0], patches), 1)
    return jnp.where(lane == index[...], 1.0, 0.0).astype(BF16)


def reg_attn_kernel(
    vis, state, seen, masked, pos, token, own_qkv, oth_qkv, own_proj, oth_proj, own_bias, oth_bias,
    gains, shifts,
    context, y1, act3_t, act4_t, query, kv, chance, mixed, branch, weight,
    act3_s, act4_s, u_s, picked,
):
    rows, width = state.shape
    images = rows // vis
    patches = pos.shape[0]
    high = pos[...].astype(BF16)
    rest = (pos[...] - high.astype(F32)).astype(BF16)
    table = jnp.concatenate([high, rest], axis=1)
    picked[0:rows, :] = dot(one_hot(seen, patches), table)
    picked[rows:, :] = dot(one_hot(masked, patches), table)
    join_columns(weight, own_qkv, oth_qkv, 3)

    def norm_seen(at):
        c = state[at, :] + picked[at, 0:width] + picked[at, width:]
        context[at, :] = c
        unit, _ = unit_rows(c)
        act4_s[at, :] = (unit * gains[1:2, :] + shifts[1:2, :]).astype(BF16)

    rows_loop(rows, norm_seen)

    def norm_masked(c, carry):
        at = pl.ds(pl.multiple_of(c * CHUNK, 16), CHUNK)
        below = pl.ds(pl.multiple_of(rows + c * CHUNK, 16), CHUNK)
        z = token[...] + (picked[below, 0:width] + picked[below, width:])
        context[below, :] = z
        unit, _ = unit_rows(z)
        act3_s[at, :] = (unit * gains[0:1, :] + shifts[0:1, :]).astype(BF16)
        act4_s[below, :] = (unit * gains[1:2, :] + shifts[1:2, :]).astype(BF16)
        return carry

    lax.fori_loop(0, rows // CHUNK, norm_masked, 0)
    transposed(act3_t, act3_s, rows)
    transposed(act4_t, act4_s, 2 * rows)
    bias_q, bias_v = head_bias_row(own_bias, oth_bias)
    query[...] = ((dot(act3_s[...], weight[:, 0:width]) + bias_q) * HEAD_DIM**-0.5).astype(BF16)
    kv[2 * rows :, :] = jnp.zeros((16, 2 * width), BF16)
    kv[0 : 2 * rows, 0:width] = dot(act4_s[...], weight[:, width : 2 * width]).astype(BF16)
    kv[0 : 2 * rows, width:] = (dot(act4_s[...], weight[:, 2 * width :]) + bias_v).astype(BF16)
    mixed[0:16, :] = jnp.zeros((16, width), BF16)
    low = head_masks()
    pairs = width // LANES

    def image(i, carry):
        at = window(i)
        below = pl.multiple_of(rows + at, 16)
        for p in range(pairs):
            lanes = slice(p * LANES, (p + 1) * LANES)
            more = slice(width + p * LANES, width + (p + 1) * LANES)
            q = query[pl.ds(at, QUERY), lanes]
            ks0, ks1 = split_pair(kv[pl.ds(at, KEYS), lanes], low)
            km0, km1 = split_pair(kv[pl.ds(below, KEYS), lanes], low)
            scores = dot(q, jnp.concatenate([ks0, km0, ks1, km1], axis=0), 1, 1)
            chosen = softmax_blocks(scores, i, vis, 2)
            chance[i * pairs + p] = chosen
            vs0, vs1 = split_pair(kv[pl.ds(at, KEYS), more], low)
            vm0, vm1 = split_pair(kv[pl.ds(below, KEYS), more], low)
            out = dot(chosen, jnp.concatenate([vs0, vm0, vs1, vm1], axis=0)).astype(BF16)
            put_window(mixed, at, lanes, out)
        return carry

    lax.fori_loop(0, images, image, 0)
    half = own_proj.shape[0]
    u_s[...] = dot(mixed[:, 0:half], own_proj[...]) + dot(mixed[:, half:], oth_proj[...])

    def finish(c, carry):
        at = pl.ds(pl.multiple_of(c * CHUNK, 16), CHUNK)
        below = pl.ds(pl.multiple_of(rows + c * CHUNK, 16), CHUNK)
        u = u_s[at, :]
        branch[at, :] = u.astype(BF16)
        y1[at, :] = context[below, :] + gains[3:4, :] * (u + shifts[3:4, :])
        return carry

    lax.fori_loop(0, rows // CHUNK, finish, 0)


def reg_ffn_kernel(
    tp, cot_hbm, y1, own_fc1, oth_fc1, own_b1, oth_b1, own_fc2, oth_fc2, gains, shifts,
    predicted, d_state, own_out, oth_out, small,
    act_s, act_t, hid, slope, d_before, u_s, cot_s, d_low, sums, sem,
):
    rows, width = y1.shape
    start = pl.multiple_of(tp[0] * rows, 16)
    copy = pltpu.make_async_copy(cot_hbm.at[pl.ds(start, rows), :], cot_s, sem)
    copy.start()
    sums[...] = jnp.zeros_like(sums)

    def norm(at):
        unit, _ = unit_rows(y1[at, :])
        act_s[at, :] = (unit * gains[2:3, :] + shifts[2:3, :]).astype(BF16)

    rows_loop(rows, norm)
    transposed(act_t, act_s, rows)
    u_s[...] = feed_forward(act_s, own_fc1, oth_fc1, own_b1, oth_b1, own_fc2, oth_fc2, hid, slope)
    copy.wait()

    def finish(at):
        branch = u_s[at, :] + shifts[4:5, :]
        predicted[at, :] = (y1[at, :] + gains[4:5, :] * branch).astype(BF16)
        grad = cot_s[at, :].astype(F32)
        sums[0:8, :] += fold(grad * branch)
        sums[8:16, :] += fold(grad)
        d_low[at, :] = (grad * gains[4:5, :]).astype(BF16)

    rows_loop(rows, finish)
    small[...] = jnp.zeros_like(small)

    def bias(k, row):
        small[8 + k : 9 + k, :] = row

    u_s[...] = feed_forward_back(
        d_low, act_t, own_fc1, oth_fc1, own_fc2, oth_fc2, hid, slope, d_before, own_out, oth_out, bias
    )

    def back(at):
        unit, scale = unit_rows(y1[at, :])
        grad = u_s[at, :]
        sums[16:24, :] += fold(grad * unit)
        sums[24:32, :] += fold(grad)
        d_state[at, :] = cot_s[at, :].astype(F32) + norm_back(grad, unit, scale, gains[2:3, :])

    rows_loop(rows, back)
    small[0:1, :] = total(sums[0:8, :])
    small[1:2, :] = total(sums[8:16, :]) * gains[4:5, :]
    small[2:3, :] = total(sums[16:24, :])
    small[3:4, :] = total(sums[24:32, :])


def pack_heads(grad, own_out, oth_out, at_q, at_v):
    width = grad.shape[0]
    half = width // 2
    for side, out in ((0, own_out), (1, oth_out)):
        lanes = slice(side * half, (side + 1) * half)
        q = grad[:, 0:width][:, lanes]
        k = grad[:, width : 2 * width][:, lanes]
        v = grad[:, 2 * width :][:, lanes]
        out[at_q : at_q + width, :] = jnp.concatenate([q, k], axis=1).astype(BF16)
        out[at_v : at_v + half, :] = jnp.concatenate([v[:half], v[half:]], axis=1).astype(BF16)


def pack_small(small, own_out, oth_out, bias_q, bias_v, ffn_small, at):
    width = small.shape[1]
    half = width // 2
    n_b1 = 2
    for side, out in ((0, own_out), (1, oth_out)):
        lanes = slice(side * half, (side + 1) * half)
        small[at : at + 1, :] = jnp.concatenate([bias_q[:, lanes], bias_v[:, lanes]], axis=1)
        small[at + 1 : at + 1 + n_b1, :] = ffn_small[8 + side * n_b1 : 8 + (side + 1) * n_b1, :]
        out[2 * width : 2 * width + small.shape[0], :] = small[...].astype(BF16)


def reg_attn_back_kernel(
    vis, patches, tp, cot_hbm, d_state, branch, mixed, query, kv, chance, weight, own_proj, oth_proj,
    context, act3_t, act4_t, seen, masked, gains, shifts, ffn_small,
    d_enc, own_out, oth_out,
    cot_s, d_low, d_mixed, d_query, d_kv, u_s, grads, sums, d_ctx, small, sem,
):
    rows, width = d_state.shape
    images = rows // vis
    start = pl.multiple_of(tp[0] * rows, 16)
    copy = pltpu.make_async_copy(cot_hbm.at[pl.ds(start, rows), :], cot_s, sem)
    copy.start()
    sums[...] = jnp.zeros_like(sums)

    def first(at):
        grad = d_state[at, :]
        sums[0:8, :] += fold(grad * (branch[at, :].astype(F32) + shifts[3:4, :]))
        sums[8:16, :] += fold(grad)
        d_low[at, :] = (grad * gains[3:4, :]).astype(BF16)

    rows_loop(rows, first)
    half = own_proj.shape[0]
    low_grad = d_low[...]
    own_out[width + half : 2 * width, :] = dot(mixed[:, 0:half], low_grad, 0, 0).astype(BF16)
    oth_out[width + half : 2 * width, :] = dot(mixed[:, half:], low_grad, 0, 0).astype(BF16)
    joined = jnp.concatenate([own_proj[...], oth_proj[...]], axis=0)
    d_mixed[...] = dot(low_grad, joined, 1, 1).astype(BF16)
    d_query[0:16, :] = jnp.zeros((16, width), BF16)
    d_kv[0:16, :] = jnp.zeros((16, 2 * width), BF16)
    d_kv[rows : rows + 16, :] = jnp.zeros((16, 2 * width), BF16)
    low = head_masks()
    low_q = low[:QUERY]
    pairs = width // LANES

    def image(i, carry):
        at = window(i)
        below = pl.multiple_of(rows + at, 16)
        for p in range(pairs):
            lanes = slice(p * LANES, (p + 1) * LANES)
            more = slice(width + p * LANES, width + (p + 1) * LANES)
            chosen = chance[i * pairs + p]
            grad_out = d_mixed[pl.ds(at, QUERY), lanes]
            vs0, vs1 = split_pair(kv[pl.ds(at, KEYS), more], low)
            vm0, vm1 = split_pair(kv[pl.ds(below, KEYS), more], low)
            d_score = attend_back(
                chosen, grad_out, jnp.concatenate([vs0, vm0, vs1, vm1], axis=0), 2
            )
            ks0, ks1 = split_pair(kv[pl.ds(at, KEYS), lanes], low)
            km0, km1 = split_pair(kv[pl.ds(below, KEYS), lanes], low)
            d_q = dot(d_score, jnp.concatenate([ks0, km0, ks1, km1], axis=0)) * HEAD_DIM**-0.5
            put_window(d_query, at, lanes, d_q.astype(BF16))
            d_k = dot(d_score, query[pl.ds(at, QUERY), lanes], 0, 0)
            d_v = dot(chosen, grad_out, 0, 0)
            for d, to in ((d_k, lanes), (d_v, more)):
                put_window(
                    d_kv, at, to, jnp.where(low_q, d[0:QUERY], d[2 * KEYS : 2 * KEYS + QUERY]).astype(BF16)
                )
                put_window(
                    d_kv, below, to,
                    jnp.where(low_q, d[KEYS : KEYS + QUERY], d[3 * KEYS : 3 * KEYS + QUERY]).astype(BF16),
                )
        return carry

    lax.fori_loop(0, images, image, 0)
    g = dot(act3_t[...], d_query[...])
    grads[:, 0:width] = g[:width]
    bias_q = g[width : width + 1]
    for c in range(2):
        g = dot(act4_t[...], d_kv[:, c * width : (c + 1) * width])
        grads[:, (c + 1) * width : (c + 2) * width] = g[:width]
        bias_v = g[width : width + 1]
    pack_heads(grads, own_out, oth_out, 0, width)
    u_s[0 : 2 * rows, :] = dot(d_kv[...], weight[:, width:], 1, 1)
    u_s[2 * rows :, :] = dot(d_query[...], weight[:, 0:width], 1, 1)
    copy.wait()

    def seen_rows(at):
        unit, scale = unit_rows(context[at, :])
        grad = u_s[at, :]
        sums[16:24, :] += fold(grad * unit)
        sums[24:32, :] += fold(grad)
        d_c = norm_back(grad, unit, scale, gains[1:2, :])
        high = d_c.astype(BF16)
        d_ctx[at, 0:width] = high
        d_ctx[at, width:] = (d_c - high.astype(F32)).astype(BF16)
        d_enc[at, :] = cot_s[at, :].astype(F32) + d_c

    rows_loop(rows, seen_rows)

    def masked_rows(c, carry):
        at = pl.ds(pl.multiple_of(c * CHUNK, 16), CHUNK)
        below = pl.ds(pl.multiple_of(rows + c * CHUNK, 16), CHUNK)
        last = pl.ds(pl.multiple_of(2 * rows + c * CHUNK, 16), CHUNK)
        unit, scale = unit_rows(context[below, :])
        grad4 = u_s[below, :]
        grad3 = u_s[last, :]
        sums[16:24, :] += fold(grad4 * unit)
        sums[24:32, :] += fold(grad4)
        sums[32:40, :] += fold(grad3 * unit)
        sums[40:48, :] += fold(grad3)
        d_z = d_state[at, :] + norm_back(
            grad3 * gains[0:1, :] + grad4 * gains[1:2, :], unit, scale, 1.0
        )
        sums[48:56, :] += fold(d_z)
        high = d_z.astype(BF16)
        d_ctx[below, 0:width] = high
        d_ctx[below, width:] = (d_z - high.astype(F32)).astype(BF16)
        return carry

    lax.fori_loop(0, rows // CHUNK, masked_rows, 0)
    pick = one_hot(seen, patches)
    both = dot(pick, d_ctx[0:rows, :], 0, 0)
    both = both + dot(one_hot(masked, patches), d_ctx[rows:, :], 0, 0)
    small[...] = jnp.zeros_like(small)
    small[0:1, :] = total(sums[32:40, :])
    small[1:2, :] = total(sums[16:24, :])
    small[2:3, :] = ffn_small[2:3, :]
    small[3:4, :] = total(sums[0:8, :])
    small[4:5, :] = ffn_small[0:1, :]
    small[5:6, :] = total(sums[40:48, :])
    small[6:7, :] = total(sums[24:32, :])
    small[7:8, :] = ffn_small[3:4, :]
    small[8:9, :] = total(sums[8:16, :]) * gains[3:4, :]
    small[9:10, :] = ffn_small[1:2, :]
    small[10:11, :] = total(sums[48:56, :])
    pack_small(small, own_out, oth_out, bias_q, bias_v, ffn_small, 11)
    after = 2 * width + 32
    d_pos = (both[:, 0:width] + both[:, width:]).astype(BF16)
    pad = jnp.zeros((own_out.shape[0] - after - patches, width), BF16)
    for out in (own_out, oth_out):
        out[after:, :] = jnp.concatenate([d_pos, pad], axis=0)


def enc_ffn_back_kernel(
    d_enc, x1, branch, act_t, hid, slope, own_fc1, oth_fc1, own_fc2, oth_fc2, gains, shifts,
    d_state, own_out, oth_out, small,
    d_low, d_before, u_s, sums,
):
    rows, width = d_enc.shape
    sums[...] = jnp.zeros_like(sums)

    def first(at):
        grad = d_enc[at, :]
        sums[0:8, :] += fold(grad * (branch[at, :].astype(F32) + shifts[3:4, :]))
        sums[8:16, :] += fold(grad)
        d_low[at, :] = (grad * gains[3:4, :]).astype(BF16)

    rows_loop(rows, first)
    small[...] = jnp.zeros_like(small)

    def bias(k, row):
        small[8 + k : 9 + k, :] = row

    u_s[...] = feed_forward_back(
        d_low, act_t, own_fc1, oth_fc1, own_fc2, oth_fc2, hid, slope, d_before, own_out, oth_out, bias
    )

    def back(at):
        unit, scale = unit_rows(x1[at, :])
        grad = u_s[at, :]
        sums[16:24, :] += fold(grad * unit)
        sums[24:32, :] += fold(grad)
        d_state[at, :] = d_enc[at, :] + norm_back(grad, unit, scale, gains[1:2, :])

    rows_loop(rows, back)
    small[0:1, :] = total(sums[0:8, :])
    small[1:2, :] = total(sums[8:16, :]) * gains[3:4, :]
    small[2:3, :] = total(sums[16:24, :])
    small[3:4, :] = total(sums[24:32, :])


def enc_attn_back_kernel(
    vis, tp, x_hbm, d_state, branch, mixed, qkv, chance, weight, own_proj, oth_proj, act_t, gains,
    shifts, ffn_small,
    own_out, oth_out, d_input,
    x_s, u_s, d_qkv, d_low, d_mixed, grads, sums, small, sem,
):
    rows, width = d_state.shape
    images = rows // vis
    start = pl.multiple_of(tp[0] * rows, 16)
    copy = pltpu.make_async_copy(x_hbm.at[pl.ds(start, rows), :], x_s, sem)
    copy.start()
    sums[...] = jnp.zeros_like(sums)

    def first(at):
        grad = d_state[at, :]
        sums[0:8, :] += fold(grad * (branch[at, :].astype(F32) + shifts[2:3, :]))
        sums[8:16, :] += fold(grad)
        d_low[at, :] = (grad * gains[2:3, :]).astype(BF16)

    rows_loop(rows, first)
    half = own_proj.shape[0]
    low_grad = d_low[...]
    own_out[width + half : 2 * width, :] = dot(mixed[:, 0:half], low_grad, 0, 0).astype(BF16)
    oth_out[width + half : 2 * width, :] = dot(mixed[:, half:], low_grad, 0, 0).astype(BF16)
    joined = jnp.concatenate([own_proj[...], oth_proj[...]], axis=0)
    d_mixed[...] = dot(low_grad, joined, 1, 1).astype(BF16)
    d_qkv[0:16, :] = jnp.zeros((16, 3 * width), BF16)
    low = head_masks()
    low_q = low[:QUERY]
    pairs = width // LANES

    def image(i, carry):
        at = window(i)
        for p in range(pairs):
            lanes = slice(p * LANES, (p + 1) * LANES)
            key = slice(width + p * LANES, width + (p + 1) * LANES)
            value = slice(2 * width + p * LANES, 2 * width + (p + 1) * LANES)
            chosen = chance[i * pairs + p]
            grad_out = d_mixed[pl.ds(at, QUERY), lanes]
            v_stack = jnp.concatenate(split_pair(qkv[pl.ds(at, KEYS), value], low), axis=0)
            d_score = attend_back(chosen, grad_out, v_stack, 1)
            k_stack = jnp.concatenate(split_pair(qkv[pl.ds(at, KEYS), key], low), axis=0)
            put_window(d_qkv, at, lanes, (dot(d_score, k_stack) * HEAD_DIM**-0.5).astype(BF16))
            d_k = dot(d_score, qkv[pl.ds(at, QUERY), lanes], 0, 0)
            d_v = dot(chosen, grad_out, 0, 0)
            for d, to in ((d_k, key), (d_v, value)):
                put_window(
                    d_qkv, at, to, jnp.where(low_q, d[0:QUERY], d[KEYS : KEYS + QUERY]).astype(BF16)
                )
        return carry

    lax.fori_loop(0, images, image, 0)
    biases = []
    for c in range(3):
        g = dot(act_t[...], d_qkv[:, c * width : (c + 1) * width])
        grads[:, c * width : (c + 1) * width] = g[:width]
        biases.append(g[width : width + 1])
    pack_heads(grads, own_out, oth_out, 0, width)
    u_s[...] = dot(d_qkv[...], weight[...], 1, 1)
    copy.wait()

    def back(at):
        unit, scale = unit_rows(x_s[at, :].astype(F32))
        grad = u_s[at, :]
        sums[16:24, :] += fold(grad * unit)
        sums[24:32, :] += fold(grad)
        d_input[at, :] = d_state[at, :] + norm_back(grad, unit, scale, gains[0:1, :])

    rows_loop(rows, back)
    small[...] = jnp.zeros_like(small)
    small[0:1, :] = total(sums[16:24, :])
    small[1:2, :] = ffn_small[2:3, :]
    small[2:3, :] = total(sums[0:8, :])
    small[3:4, :] = ffn_small[0:1, :]
    small[4:5, :] = total(sums[24:32, :])
    small[5:6, :] = ffn_small[3:4, :]
    small[6:7, :] = total(sums[8:16, :]) * gains[2:3, :]
    small[7:8, :] = ffn_small[1:2, :]
    pack_small(small, own_out, oth_out, biases[0], biases[2], ffn_small, 8)
    pad = jnp.zeros((own_out.shape[0] - 2 * width - small.shape[0], width), BF16)
    own_out[2 * width + small.shape[0] :, :] = pad
    oth_out[2 * width + small.shape[0] :, :] = pad


def halve_kernel(step, place, mine, got, keep, send):
    half = keep.shape[0]
    bit = place[step]
    at = pl.ds(pl.multiple_of(bit * half, 16), half)
    to = pl.ds(pl.multiple_of((1 - bit) * half, 16), half)
    keep[...] = (mine[at, :].astype(F32) + got[at, :].astype(F32)).astype(BF16)
    send[...] = (mine[to, :].astype(F32) + got[to, :].astype(F32)).astype(BF16)


def add_kernel(mine, got, out):
    out[...] = (mine[...].astype(F32) + got[...].astype(F32)).astype(BF16)


def join_kernel(step, place, mine, got, out):
    half = mine.shape[0]
    bit = place[step]
    out[pl.ds(pl.multiple_of(bit * half, 16), half), :] = mine[...]
    out[pl.ds(pl.multiple_of((1 - bit) * half, 16), half), :] = got[...]


def ffn_out_kernel(place, mine, got, grad1, grad2):
    width = grad1.shape[0]

    def write(first, second):
        for c in range(grad1.shape[1] // width):
            grad1[:, c * width : (c + 1) * width] = first[c * width : (c + 1) * width, :].astype(F32)
        grad2[...] = second[...].astype(F32)

    @pl.when(place[1] == 0)
    def _():
        write(mine, got)

    @pl.when(place[1] == 1)
    def _():
        write(got, mine)


def heads_out_kernel(place, mine, got, grad_qkv, grad_proj, rest, whole):
    join_kernel(1, place, mine, got, whole)
    width = grad_qkv.shape[1]
    half = width // 2
    first = whole[0:width, :].astype(F32)
    grad_qkv[0] = first[:, :half]
    grad_qkv[1] = first[:, half:]
    value = whole[width : width + half, :].astype(F32)
    grad_qkv[2, 0:half, :] = value[:, :half]
    grad_qkv[2, half:, :] = value[:, half:]
    grad_proj[...] = whole[width + half : 2 * width, :].astype(F32)
    rest[...] = whole[2 * width :, :].astype(F32)


def run(kernel, name, ins, outs, scratch, flops, hbm=(), smem=()):
    specs = []
    for k in range(len(ins)):
        if k in smem:
            specs.append(pl.BlockSpec(memory_space=pltpu.SMEM))
        elif k in hbm:
            specs.append(pl.BlockSpec(memory_space=pl.ANY))
        else:
            specs.append(pl.BlockSpec(memory_space=pltpu.VMEM))
    shapes = [jax.ShapeDtypeStruct(s, d) for s, d in outs]
    moved = sum(a.size * a.dtype.itemsize for a in (*ins, *shapes))
    return pl.pallas_call(
        kernel,
        name=name,
        out_shape=shapes,
        in_specs=specs,
        out_specs=[pl.BlockSpec(memory_space=pltpu.VMEM)] * len(outs),
        scratch_shapes=scratch,
        compiler_params=pltpu.CompilerParams(vmem_limit_bytes=VMEM_LIMIT),
        cost_estimate=pl.CostEstimate(flops=flops, bytes_accessed=moved, transcendentals=0),
    )(*ins)


def vmem(shape, dtype):
    return pltpu.VMEM(shape, dtype)


def swap(a):
    return lax.ppermute(a, "tp", [(0, 1), (1, 0)])


AXES = ("dp", "tp")
ORDERS = ((0, 1, 2, 3), (1, 0, 3, 2))


def flip(a, step):
    n = lax.axis_size("dp")
    pairs = [
        (2 * d + t, 2 * (d ^ (1 << ORDERS[t][step])) + t) for d in range(n) for t in range(2)
    ]
    return lax.ppermute(a, AXES, pairs)


def halve(place, step, mine, got):
    shape = ((mine.shape[0] // 2, mine.shape[1]), BF16)
    return run(functools.partial(halve_kernel, step), "halve", (place, mine, got), [shape, shape], [], 0, smem=(0,))


def add(mine, got):
    return run(add_kernel, "add", (mine, got), [(mine.shape, BF16)], [], 0)[0]


def join(place, step, mine, got):
    shape = ((2 * mine.shape[0], mine.shape[1]), BF16)
    return run(functools.partial(join_kernel, step), "join", (place, mine, got), [shape], [], 0, smem=(0,))[0]


def reduce_over_dp(place, own, oth):
    if lax.axis_size("dp") != 16:
        whole = lax.psum(own.astype(F32) + swap(oth).astype(F32), "dp").astype(BF16)
        half = whole.shape[0] // 2
        first = place[1] == 0
        return (
            jnp.where(first, whole[:half], whole[half:]),
            jnp.where(first, whole[half:], whole[:half]),
        )
    keep, send = halve(place, 1, own, swap(oth))
    keep, send = halve(place, 2, keep, flip(send, 0))
    part = add(keep, flip(send, 1))
    part = add(part, flip(part, 2))
    part = add(part, flip(part, 3))
    part = join(place, 2, part, flip(part, 1))
    return part, flip(part, 0)


def body(
    x_visible,
    patch_order,
    enc_qkv,
    enc_head_bias,
    enc_proj,
    enc_fc1,
    enc_fc1_bias,
    enc_fc2,
    enc_gains,
    enc_shifts,
    reg_qkv,
    reg_head_bias,
    reg_proj,
    reg_fc1,
    reg_fc1_bias,
    reg_fc2,
    reg_gains,
    reg_shifts,
    pos_embed,
    mask_token,
    enc_cot,
    reg_cot,
):
    all_images, patches = patch_order.shape
    width = x_visible.shape[1]
    vis = x_visible.shape[0] // all_images
    images = all_images // 2
    rows = images * vis
    hidden = 2 * enc_fc1.shape[1]
    half = width // 2
    pairs = width // LANES
    tp_index = lax.axis_index("tp")
    tp = tp_index.astype(jnp.int32).reshape(1)
    dp_index = lax.axis_index("dp")
    bits = [(dp_index >> jnp.where(tp_index == 0, *(o[k] for o in ORDERS))) & 1 for k in range(2)]
    place = jnp.stack([tp_index, *bits]).astype(jnp.int32)

    enc_b1 = enc_fc1_bias.reshape(1, -1)
    reg_b1 = reg_fc1_bias.reshape(1, -1)
    oth_enc_qkv, oth_enc_proj, oth_enc_bias = swap(enc_qkv), swap(enc_proj), swap(enc_head_bias)
    oth_enc_fc1, oth_enc_fc2, oth_enc_b1 = swap(enc_fc1), swap(enc_fc2), swap(enc_b1)
    oth_reg_qkv, oth_reg_proj, oth_reg_bias = swap(reg_qkv), swap(reg_proj), swap(reg_head_bias)
    oth_reg_fc1, oth_reg_fc2, oth_reg_b1 = swap(reg_fc1), swap(reg_fc2), swap(reg_b1)
    order = lax.dynamic_slice_in_dim(patch_order, tp_index * images, images, 0)
    seen = order[:, :vis].reshape(rows, 1)
    masked = order[:, vis:].reshape(rows, 1)

    state_f = ((rows, width), F32)
    state_b = ((rows, width), BF16)
    act_t = ((width + 16, rows), BF16)
    wide = ((rows, hidden), BF16)
    layer = 2 * rows * width

    x1, act1_t, qkv1, chance1, mixed1, branch1, weight1 = run(
        functools.partial(enc_attn_kernel, vis),
        "enc_attn",
        (tp, x_visible, enc_qkv, oth_enc_qkv, enc_proj, oth_enc_proj, enc_head_bias, oth_enc_bias,
         enc_gains, enc_shifts),
        [state_f, act_t, ((rows + 16, 3 * width), BF16), ((images * pairs, QUERY, 2 * KEYS), BF16),
         state_b, state_b, ((width, 3 * width), BF16)],
        [vmem(*state_b), vmem(*state_b), vmem(*state_f), pltpu.SemaphoreType.DMA],
        layer * width * 5, hbm=(1,), smem=(0,),
    )
    enc_state, encoded, act2_t, hid2, slope2, branch2 = run(
        enc_ffn_kernel,
        "enc_ffn",
        (x1, enc_fc1, oth_enc_fc1, enc_b1, oth_enc_b1, enc_fc2, oth_enc_fc2, enc_gains, enc_shifts),
        [state_f, state_b, act_t, wide, wide, state_b],
        [vmem(*state_b), vmem(*state_f)],
        layer * hidden * 2,
    )
    context, y1, act3_t, act4_t, query3, kv3, chance3, mixed3, branch3, weight3 = run(
        functools.partial(reg_attn_kernel, vis),
        "reg_attn",
        (enc_state, seen, masked, pos_embed, mask_token.reshape(1, width), reg_qkv, oth_reg_qkv,
         reg_proj, oth_reg_proj, reg_head_bias, oth_reg_bias, reg_gains, reg_shifts),
        [((2 * rows, width), F32), state_f, act_t, ((width + 16, 2 * rows), BF16), state_b,
         ((2 * rows + 16, 2 * width), BF16), ((images * pairs, QUERY, 4 * KEYS), BF16), state_b,
         state_b, ((width, 3 * width), BF16)],
        [vmem(*state_b), vmem((2 * rows, width), BF16), vmem(*state_f),
         vmem((2 * rows, 2 * width), F32)],
        layer * width * 8,
    )
    stage = ((2 * hidden // 2, width), BF16)
    predicted, d_state3, own_a, oth_a, small_a = run(
        reg_ffn_kernel,
        "reg_ffn_both",
        (tp, reg_cot, y1, reg_fc1, oth_reg_fc1, reg_b1, oth_reg_b1, reg_fc2, oth_reg_fc2, reg_gains,
         reg_shifts),
        [state_b, state_f, stage, stage, ((16, width), F32)],
        [vmem(*state_b), vmem(*act_t), vmem(*wide), vmem(*wide), vmem(*wide), vmem(*state_f),
         vmem(*state_b), vmem(*state_b), vmem((32, width), F32), pltpu.SemaphoreType.DMA],
        layer * hidden * 6, hbm=(1,), smem=(0,),
    )
    heads_b = ((2 * width + 256, width), BF16)
    d_enc, own_b, oth_b = run(
        functools.partial(reg_attn_back_kernel, vis, patches),
        "reg_attn_back",
        (tp, enc_cot, d_state3, branch3, mixed3, query3, kv3, chance3, weight3, reg_proj,
         oth_reg_proj, context, act3_t, act4_t, seen, masked, reg_gains, reg_shifts, small_a),
        [state_f, heads_b, heads_b],
        [vmem(*state_b), vmem(*state_b), vmem(*state_b), vmem(*state_b),
         vmem((2 * rows, 2 * width), BF16), vmem((3 * rows, width), F32),
         vmem((width, 3 * width), F32), vmem((56, width), F32), vmem((2 * rows, 2 * width), BF16),
         vmem((32, width), F32), pltpu.SemaphoreType.DMA],
        layer * width * 16, hbm=(1,), smem=(0,),
    )
    d_state1, own_c, oth_c, small_c = run(
        enc_ffn_back_kernel,
        "enc_ffn_back",
        (d_enc, x1, branch2, act2_t, hid2, slope2, enc_fc1, oth_enc_fc1, enc_fc2, oth_enc_fc2,
         enc_gains, enc_shifts),
        [state_f, stage, stage, ((16, width), F32)],
        [vmem(*state_b), vmem(*wide), vmem(*state_f), vmem((32, width), F32)],
        layer * hidden * 4,
    )
    heads_d = ((2 * width + 64, width), BF16)
    own_d, oth_d, d_input = run(
        functools.partial(enc_attn_back_kernel, vis),
        "enc_attn_back",
        (tp, x_visible, d_state1, branch1, mixed1, qkv1, chance1, weight1, enc_proj, oth_enc_proj,
         act1_t, enc_gains, enc_shifts, small_c),
        [heads_d, heads_d, state_f],
        [vmem(*state_b), vmem(*state_f), vmem((rows, 3 * width), BF16), vmem(*state_b),
         vmem(*state_b), vmem((width, 3 * width), F32), vmem((32, width), F32),
         vmem((32, width), F32), pltpu.SemaphoreType.DMA],
        layer * width * 12, hbm=(1,), smem=(0,),
    )

    def both_halves(mine):
        theirs = swap(mine)
        return jnp.where(
            tp_index == 0,
            jnp.concatenate([mine, theirs], axis=0),
            jnp.concatenate([theirs, mine], axis=0),
        )

    encoded, predicted, d_input = both_halves(encoded), both_halves(predicted), both_halves(d_input)

    fc_shapes = [((width, hidden // 2), F32), ((hidden // 2, width), F32)]
    reg_g1, reg_g2 = run(
        ffn_out_kernel, "ffn_out", (place, *reduce_over_dp(place, own_a, oth_a)), fc_shapes, [], 0, smem=(0,)
    )
    enc_g1, enc_g2 = run(
        ffn_out_kernel, "ffn_out", (place, *reduce_over_dp(place, own_c, oth_c)), fc_shapes, [], 0, smem=(0,)
    )

    def heads_out(own, oth):
        shapes = [((3, width, half), F32), ((half, width), F32), ((own.shape[0] - 2 * width, width), F32)]
        grad_qkv, grad_proj, rest = run(
            heads_out_kernel, "heads_out", (place, *reduce_over_dp(place, own, oth)), shapes,
            [vmem(own.shape, BF16)], 0, smem=(0,),
        )
        return grad_qkv, grad_proj, rest, (rest + swap(rest)) * 0.5

    reg_gq, reg_gp, rest, mean = heads_out(own_b, oth_b)
    n_b1 = hidden // (2 * width)
    grad_reg_gains, grad_reg_shifts, grad_mask_token = mean[0:5], mean[5:10], mean[10]
    hb_reg = rest[11].reshape(2, half)
    b1_reg = rest[12 : 12 + n_b1].reshape(-1)
    grad_pos = mean[32 : 32 + patches]
    enc_gq, enc_gp, rest, mean = heads_out(own_d, oth_d)
    grad_enc_gains, grad_enc_shifts = mean[0:4], mean[4:8]
    hb_enc = rest[8].reshape(2, half)
    b1_enc = rest[9 : 9 + n_b1].reshape(-1)
    return (
        encoded, predicted, d_input, enc_gq, hb_enc, enc_gp, enc_g1, b1_enc, enc_g2, grad_enc_gains,
        grad_enc_shifts, reg_gq, hb_reg, reg_gp, reg_g1, b1_reg, reg_g2, grad_reg_gains,
        grad_reg_shifts, grad_pos, grad_mask_token,
    )


def solution(mesh):
    placed = (
        P("dp", None),
        P("dp", None),
        P(None, None, "tp"),
        P(None, "tp"),
        P("tp", None),
        P(None, "tp"),
        P("tp"),
        P("tp", None),
        P(),
        P(),
        P(None, None, "tp"),
        P(None, "tp"),
        P("tp", None),
        P(None, "tp"),
        P("tp"),
        P("tp", None),
        P(),
        P(),
        P(),
        P(),
        P("dp", None),
        P("dp", None),
    )
    return jax.shard_map(
        body,
        mesh=mesh,
        in_specs=placed,
        out_specs=(
            P("dp", None),
            P("dp", None),
            P("dp", None),
            P(None, None, "tp"),
            P(None, "tp"),
            P("tp", None),
            P(None, "tp"),
            P("tp"),
            P("tp", None),
            P(),
            P(),
            P(None, None, "tp"),
            P(None, "tp"),
            P("tp", None),
            P(None, "tp"),
            P("tp"),
            P("tp", None),
            P(),
            P(),
            P(),
            P(),
        ),
        check_vma=False,
    )
```

time: 732 us -> 319 us (0.44)
  waiting for transfers between devices: 242 us -> 32 us
  Pallas kernels: 0 us -> 205 us
  matrix products: 135 us -> 0 us
  local copies, waits for them, and re-layouts: 143 us -> 34.8 us
  other arithmetic: 104 us -> 5.21 us
  blocking collectives: 81.4 us -> 0 us
  starting transfers between devices: 1.24 us -> 35.2 us
  between operations: 16 us -> 1.16 us
    psum x8 -> x0, waiting for transfers between devices: 242 us -> none  [the longest x1 157 us: body(): lax.psum((grad_enc_qkv, grad_enc_head_bias, grad_enc_proj, grad_enc_fc1,...]
    pallas_call x0 -> x35, Pallas kernels: none -> 205 us  [run(): pl.pallas_call(kernel, name=name, out_shape=shapes, in_specs=specs, out_s...]
    dot_general x48 -> x0, matrix products: 135 us -> none  [the longest x12 51.7 us: matmul(): return jnp.dot(left_side, right_side, preferred_element_type=jnp.float32)]
    psum x1 -> x0, blocking collectives: 81.4 us -> none  [body(): lax.psum((grad_enc_qkv, grad_enc_head_bias, grad_enc_proj, grad_enc_fc1,...]
    reduce_sum x20 -> x0, other arithmetic: 54.2 us -> none  [the longest x4 14.1 us: norm_backward(): jnp.sum(grad_out * unit_rows, axis=0)]
    reshape x16 -> x7, local copies, waits for them, and re-layouts: 56 us -> 3.65 us  [the longest x1 0.95 us: body(): seen = order[:, :vis].reshape(rows, 1)]
    convert_element_type x17 -> x0, local copies, waits for them, and re-layouts: 41.1 us -> none  [the longest x4 12 us: attend_back(): grad_keys.reshape(key_rows.shape).astype(jnp.bfloat16)]
    ppermute x0 -> x45, starting transfers between devices: none -> 35.2 us  [the longest x24 29.3 us: flip(): return lax.ppermute(a, AXES, pairs)]
  transfers between devices with their start and end apart: 8 -> 45, of which waited for: 7 -> 12; matrix products, arithmetic and copies ran while one was open for 10% -> 7% of each run, Pallas kernels for 0% -> 34%
where the time goes in v1:
time: 319 us; the launch traced here: 313 us
  Pallas kernels  205 us (64%)
  starting transfers between devices  35.2 us (11%)
  local copies, waits for them, and re-layouts  34.8 us (11%)
  waiting for transfers between devices  32 us (10%)
  other arithmetic  5.21 us (2%)
    pallas_call x35, Pallas kernels, run(): pl.pallas_call(kernel, name=name, out_shape=shapes, in_specs=specs, out_s...  205 us
    ppermute x24, starting transfers between devices, flip(): return lax.ppermute(a, AXES, pairs)  29.3 us
    ppermute x24, waiting for transfers between devices, flip(): return lax.ppermute(a, AXES, pairs)  27.1 us
    unnamed x106, local copies, waits for them, and re-layouts  24.3 us
  transfers between devices with their start and end apart: 45, of which 12 were waited for; matrix products, arithmetic and copies ran while one was open for 7% of the time, Pallas kernels for 34%

profile of v1, /device:TPU:0, one launch (start us, length us, event | category | flops | bytes accessed | tf_op | source)
XLA Modules:
  0.0 313.2 jit_solution(17983016816655714314)
XLA Ops:
  2.2 2.9 collective-permute-done.2.oth_bias
  5.5 1.2 collective-permute-done.1.oth_proj
  7.3 2.1 copy.59.own_qkv
  14.4 15.7 %enc_attn.1 = (f32[784,384]{1,0:T(8,128)}, bf16[400,784]{1,0:T(8,128)(2,1)}, bf16[800,1152]{1,0:T(8,128)(2,1)}, bf16[24,112,256]{2,1,0:T(8,128)(2,1)}, bf16[784,...) custom-call(s32[1]{0:T(128)} %bitcast.tp, bf16[1568,384]{1,0:T(8,128)(2,1)} %x_hbm.3, ...), custom_call_target="tpu_custom_call" | custom-call | flops 1156055040 | bytes 9539076 | tf_op jit(solution)/shard_map/enc_attn/pallas_call | solution.py:740
  32.7 13.9 %enc_ffn.1 = (f32[784,384]{1,0:T(8,128)}, bf16[784,384]{1,0:T(8,128)(2,1)}, bf16[400,784]{1,0:T(8,128)(2,1)}, bf16[784,1536]{1,0:T(8,128)(2,1)}, bf16[784,1536]{1,0:T(8,128)(2,1)}, /*index=5*/bf16[784,384]{1,0:T(8,128)(2,1)}) custom-call(f32[784,384]{1,0:T(8,128)} %get-tuple-element.85.x1, bf16[384,768]{1,0:T(8,128)(2,1)} %own_fc1.5, ...), custom_call_target="tpu_custom_call" | custom-call | flops 1849688064 | bytes 11434496 | tf_op jit(solution)/shard_map/enc_ffn/pallas_call | solution.py:740
  47.4 22.9 %reg_attn.1 = (f32[1568,384]{1,0:T(8,128)}, f32[784,384]{1,0:T(8,128)}, bf16[400,784]{1,0:T(8,128)(2,1)}, bf16[400,1568]{1,0:T(8,128)(2,1)}, bf16[784,384]{1,0:T...) custom-call(f32[784,384]{1,0:T(8,128)} %get-tuple-element.87.state, ...), custom_call_target="tpu_custom_call" | custom-call | flops 1849688064 | bytes 16082048 | tf_op jit(solution)/shard_map/reg_attn/pallas_call | solution.py:740
  71.2 22.3 %reg_ffn_both.1 = (bf16[784,384]{1,0:T(8,128)(2,1)}, f32[784,384]{1,0:T(8,128)}, bf16[1536,384]{1,0:T(8,128)(2,1)}, bf16[1536,384]{1,0:T(8,128)(2,1)}, f32[16,384]{1,0:T(8,128)}) custom-call(s32[1]{0:T(128)} %bitcast.tp, bf16[1568,384]{1,0:T(8,128)(2,1)} %cot_hbm.2, f32[784,384]{1,0:T(8,128)} %get-tuple-element.88.y1, bf16[384,768]{1,0:T(8,128)(2,1)} %own_fc1.4, ...), custom_call_target="tpu_custom_call" | custom-call | flops 5549064192 | bytes 8979460 | tf_op jit(solution)/shard_map/reg_ffn_both/pallas_call | solution.py:740
  93.4 27.5 %reg_attn_back.1 = (f32[784,384]{1,0:T(8,128)}, bf16[1024,384]{1,0:T(8,128)(2,1)}, bf16[1024,384]{1,0:T(8,128)(2,1)}) custom-call(s32[1]{0:T(128)} %bitcast.tp, bf16[1568,384]{1,0:T(8,128)(2,1)} %cot_hbm.3, f32[784,384]{1,0:T(8,128)} %get-tuple-element.90.d_state, bf16[784,384]{1,0:T(8,128)(2,1)} %get-tuple-element.91.branch, ...), custom_call_target="tpu_custom_call" | custom-call | flops 3699376128 | bytes 17693316 | tf_op jit(solution)/shard_map/reg_attn_back/pallas_call | solution.py:740
  120.9 25.3 %enc_ffn_back.1 = (f32[784,384]{1,0:T(8,128)}, bf16[1536,384]{1,0:T(8,128)(2,1)}, bf16[1536,384]{1,0:T(8,128)(2,1)}, f32[16,384]{1,0:T(8,128)}) custom-call(f32[784,384]{1,0:T(8,128)} %get-tuple-element.101.d_enc, f32[784,384]{1,0:T(8,128)} %get-tuple-element.85.x1, bf16[784,384]{1,0:T(8,128)(2,1)} %get-tuple-element.102.branch, ...), custom_call_target="tpu_custom_call" | custom-call | flops 3699376128 | bytes 14414336 | tf_op jit(solution)/shard_map/enc_ffn_back/pallas_call | solution.py:740
  146.2 19.5 %enc_attn_back.1 = (bf16[832,384]{1,0:T(8,128)(2,1)}, bf16[832,384]{1,0:T(8,128)(2,1)}, f32[784,384]{1,0:T(8,128)}) custom-call(s32[1]{0:T(128)} %bitcast.tp, bf16[1568,384]{1,0:T(8,128)(2,1)} %x_hbm.3, f32[784,384]{1,0:T(8,128)} %get-tuple-element.106.d_state, bf16[784,384]{1,0:T(8,128)(2,1)} %get-tuple-element.107.branch, ...), custom_call_target="tpu_custom_call" | custom-call | flops 2774532096 | bytes 11158020 | tf_op jit(solution)/shard_map/enc_attn_back/pallas_call | solution.py:740
  168.1 2.2 halve.8
  170.3 2.6 collective-permute-start.16
  173.9 2.4 halve.12
  176.2 1.9 collective-permute-done.16.got
  178.9 1.8 halve.9
  180.7 2.1 collective-permute-start.17
  182.8 3.5 %collective-permute-done.17.got = bf16[208,384]{1,0:T(8,128)(2,1)S(1)} collective-permute-done((bf16[208,384]{1,0:T(8,128)(2,1)}, bf16[208,384]{1,0:T(8,128)(2,1)S(1)}, u32[]{:S(2)}, u32[]{:S(2)}) %collective-permute-start.17) | collective-permute-done | bytes 159776 | tf_op jit(solution)/shard_map/ppermute | solution.py:769
  186.9 1.7 add.34.mine
  188.6 2.1 collective-permute-start.18
  191.4 1.9 halve.13
  193.3 1.5 collective-permute-start.32
  195.9 2.9 halve.14
  198.8 1.5 collective-permute-start.38
  201.0 1.7 add.35.mine
  202.7 2.6 collective-permute-start.19
  206.3 2.9 halve.10
  209.8 1.7 add.40.mine
  212.0 7.1 %collective-permute-done.33.got = bf16[256,384]{1,0:T(8,128)(2,1)S(1)} collective-permute-done((bf16[256,384]{1,0:T(8,128)(2,1)}, bf16[256,384]{1,0:T(8,128)(2,1)S(1)}, u32[]{:S(2)}, u32[]{:S(2)}) %collective-permute-start.33) | collective-permute-done | bytes 196640 | tf_op jit(solution)/shard_map/ppermute | solution.py:769
  219.7 1.7 add.36.mine
  221.4 1.1 collective-permute-start.20
  222.6 1.7 add.41.mine
  224.3 2.1 halve.15
  227.3 2.1 halve.11
  231.5 1.5 maximum_select_fusion.2
  232.9 1.8 join.4.mine
  235.8 1.7 add.42.mine
  237.6 1.2 collective-permute-start.35
  238.8 1.5 maximum_select_fusion.1
  240.3 4.8 %collective-permute-done.35.got = bf16[256,384]{1,0:T(8,128)(2,1)S(1)} collective-permute-done((bf16[256,384]{1,0:T(8,128)(2,1)}, bf16[256,384]{1,0:T(8,128)(2,1)S(1)}, u32[]{:S(2)}, u32[]{:S(2)}) %collective-permute-start.35) | collective-permute-done | bytes 196640 | tf_op jit(solution)/shard_map/ppermute | solution.py:769
  245.7 1.8 join.6.mine
  248.8 1.8 add.43.mine
  251.7 1.8 add.37.mine
  253.5 1.7 collective-permute-start.25
  255.2 1.6 maximum_select_fusion
  257.5 2.4 heads_out.2
  260.6 2.5 copy.67
  264.5 1.8 add.44.mine
  266.3 2.2 collective-permute-start.41
  269.2 1.8 add.38.mine
  273.2 2.5 heads_out.3
  275.8 1.6 collective-permute-done.41.got
  278.2 1.9 add.45.mine
  280.0 1.6 collective-permute-start.42
  281.6 1.8 collective-permute-done.26.got
  284.1 1.8 add.39.mine
  285.9 1.2 collective-permute-start.27
  287.8 1.3 copy.68
  291.0 1.9 join.7.mine
  293.0 1.2 collective-permute-start.43
  294.9 2.0 join.5.mine
  299.7 3.4 %collective-permute-done.43.got = bf16[768,384]{1,0:T(8,128)(2,1)S(1)} collective-permute-done((bf16[768,384]{1,0:T(8,128)(2,1)}, bf16[768,384]{1,0:T(8,128)(2,1)S(1)}, u32[]{:S(2)}, u32[]{:S(2)}) %collective-permute-start.43) | collective-permute-done | bytes 589856 | tf_op jit(solution)/shard_map/ppermute | solution.py:769
  303.9 2.8 ffn_out.3
  306.7 2.7 collective-permute-done.28.got
  310.2 2.8 ffn_out.2
  (193 shorter events, 43.4 us)
Async XLA Ops:
  0.7 8.7 %copy-start.11 = (bf16[3,384,192]{1,2,0:T(8,128)(2,1)S(1)}, bf16[3,384,192]{1,2,0:T(8,128)(2,1)}, u32[]{:S(2)}) copy-start(bf16[3,384,192]{1,2,0:T(8,128)(2,1)} %param.32) | copy-start | bytes 1327108
  0.7 9.8 %copy-start.36 = (f32[768]{0:T(1024)S(1)}, f32[768]{0:T(1024)}, u32[]{:S(2)}) copy-start(f32[768]{0:T(1024)} %param.28) | copy-start | bytes 9220
  0.7 9.8 %copy-start.38 = (s32[16,196]{1,0:T(8,128)S(1)}, s32[16,196]{1,0:T(8,128)}, u32[]{:S(2)}) copy-start(s32[16,196]{1,0:T(8,128)} %param.23) | copy-start | bytes 37636
  0.7 6.4 %collective-permute-start = (bf16[3,384,192]{1,2,0:T(8,128)(2,1)}, bf16[3,384,192]{1,2,0:T(8,128)(2,1)S(1)}, u32[]{:S(2)}, u32[]{:S(2)}) collective-permute-start(bf16[3,384,192]{1,2,0:T(8,128)(2,1)} %param.24), channel_id=1, source_target_pairs={{0,1},{1,0},{2,3},{3,2},{4,5},{5,4},{6,7},{7,6},{8,9},{9,8},{10,11... | collective-permute-start | bytes 1327112 | tf_op jit(solution)/shard_map/ppermute | solution.py:757
  1.2 30.2 %collective-permute-start.3 = (bf16[384,768]{1,0:T(8,128)(2,1)}, bf16[384,768]{1,0:T(8,128)(2,1)S(1)}, u32[]{:S(2)}, u32[]{:S(2)}) collective-permute-start(bf16[384,768]{1,0:T(8,128)(2,1)} %own_fc1.5), channel_id=1, source_target_pairs={{0,1},{1,0},{2,3},{3,2},{4,5},{5,4},{6,7},{7,6},{8,9},{9,8},{10,11... | collective-permute-start | bytes 1769480 | tf_op jit(solution)/shard_map/ppermute | solution.py:757
  1.3 30.6 %collective-permute-start.5 = (bf16[768,384]{1,0:T(8,128)(2,1)}, bf16[768,384]{1,0:T(8,128)(2,1)S(1)}, u32[]{:S(2)}, u32[]{:S(2)}) collective-permute-start(bf16[768,384]{1,0:T(8,128)(2,1)} %own_fc2.5), channel_id=1, source_target_pairs={{0,1},{1,0},{2,3},{3,2},{4,5},{5,4},{6,7},{7,6},{8,9},{9,8},{10,11... | collective-permute-start | bytes 1769480 | tf_op jit(solution)/shard_map/ppermute | solution.py:757
  1.7 12.3 %collective-permute-start.7 = (bf16[3,384,192]{1,2,0:T(8,128)(2,1)}, bf16[3,384,192]{1,2,0:T(8,128)(2,1)S(1)}, u32[]{:S(2)}, u32[]{:S(2)}) collective-permute-start(bf16[3,384,192]{1,2,0:T(8,128)(2,1)} %param.32), channel_id=1, source_target_pairs={{0,1},{1,0},{2,3},{3,2},{4,5},{5,4},{6,7},{7,6},{8,9},{9,8},{10,11... | collective-permute-start | bytes 1327112 | tf_op jit(solution)/shard_map/ppermute | solution.py:757
  1.8 3.4 %collective-permute-start.2 = (f32[2,192]{1,0:T(2,128)}, f32[2,192]{1,0:T(2,128)S(1)}, u32[]{:S(2)}, u32[]{:S(2)}) collective-permute-start(f32[2,192]{1,0:T(2,128)} %own_bias.2), channel_id=1, source_target_pairs={{0,1},{1,0},{2,3},{3,2},{4,5},{5,4},{6,7},{7,6},{8,9},{9,8},{10,11... | collective-permute-start | bytes 4616 | tf_op jit(solution)/shard_map/ppermute | solution.py:757
  5.2 6.3 %copy-start.49 = (f32[2,192]{1,0:T(2,128)}, f32[2,192]{1,0:T(2,128)S(1)}, u32[]{:S(2)}) copy-start(f32[2,192]{1,0:T(2,128)S(1)} %collective-permute-done.2.oth_bias) | copy-start | bytes 4612
  5.2 1.6 collective-permute-start.1
  6.8 4.7 %copy-start.45 = (bf16[192,384]{1,0:T(8,128)(2,1)}, bf16[192,384]{1,0:T(8,128)(2,1)S(1)}, u32[]{:S(2)}) copy-start(bf16[192,384]{1,0:T(8,128)(2,1)S(1)} %collective-permute-done.1.oth_proj) | copy-start | bytes 442372
  6.8 63.6 %collective-permute-start.10 = (bf16[384,768]{1,0:T(8,128)(2,1)}, bf16[384,768]{1,0:T(8,128)(2,1)S(1)}, u32[]{:S(2)}, u32[]{:S(2)}) collective-permute-start(bf16[384,768]{1,0:T(8,128)(2,1)} %own_fc1.4), channel_id=1, source_target_pairs={{0,1},{1,0},{2,3},{3,2},{4,5},{5,4},{6,7},{7,6},{8,9},{9,8},{10,11... | collective-permute-start | bytes 1769480 | tf_op jit(solution)/shard_map/ppermute | solution.py:757
  7.1 63.2 %collective-permute-start.12 = (bf16[768,384]{1,0:T(8,128)(2,1)}, bf16[768,384]{1,0:T(8,128)(2,1)}, u32[]{:S(2)}, u32[]{:S(2)}) collective-permute-start(bf16[768,384]{1,0:T(8,128)(2,1)} %own_fc2.4), channel_id=1, source_target_pairs={{0,1},{1,0},{2,3},{3,2},{4,5},{5,4},{6,7},{7,6},{8,9},{9,8},{10,11... | collective-permute-start | bytes 1769480 | tf_op jit(solution)/shard_map/ppermute | solution.py:757
  7.3 5.2 %copy-start.41 = (f32[384]{0:T(512)S(1)}, f32[384]{0:T(512)}, u32[]{:S(2)}) copy-start(f32[384]{0:T(512)} %param.41) | copy-start | bytes 4612
  7.3 5.7 %copy-start.37 = (f32[768]{0:T(1024)S(1)}, f32[768]{0:T(1024)}, u32[]{:S(2)}) copy-start(f32[768]{0:T(1024)} %param.36) | copy-start | bytes 9220
  10.4 19.7 %copy-start.40 = (f32[1,768]{1,0:T(1,128)}, f32[1,768]{1,0:T(1,128)S(1)}, u32[]{:S(2)}) copy-start(f32[1,768]{1,0:T(1,128)S(1)} %reshape.67.own_b1) | copy-start | bytes 9220
  13.0 18.9 %copy-start.39 = (f32[1,768]{1,0:T(1,128)}, f32[1,768]{1,0:T(1,128)S(1)}, u32[]{:S(2)}) copy-start(f32[1,768]{1,0:T(1,128)S(1)} %reshape.71.own_b1) | copy-start | bytes 9220
  14.1 17.1 %collective-permute-start.4 = (f32[1,768]{1,0:T(1,128)S(1)}, f32[1,768]{1,0:T(1,128)S(1)}, u32[]{:S(2)}, u32[]{:S(2)}) collective-permute-start(f32[1,768]{1,0:T(1,128)S(1)} %reshape.67.own_b1), channel_id=1, source_target_pairs={{0,1},{1,0},{2,3},{3,2},{4,5},{5,4},{6,7},{7,6},{8,9},{9,8},{10,11... | collective-permute-start | bytes 9224 | tf_op jit(solution)/shard_map/ppermute | solution.py:757
  14.4 16.8 %copy-start.33 = (bf16[192,384]{1,0:T(8,128)(2,1)S(1)}, bf16[192,384]{1,0:T(8,128)(2,1)}, u32[]{:S(2)}) copy-start(bf16[192,384]{1,0:T(8,128)(2,1)} %own_proj.6) | copy-start | bytes 442372
  14.4 17.0 %copy-start.48 = (f32[2,192]{1,0:T(2,128)S(1)}, f32[2,192]{1,0:T(2,128)}, u32[]{:S(2)}) copy-start(f32[2,192]{1,0:T(2,128)} %own_bias.3) | copy-start | bytes 4612
  31.2 15.5 %collective-permute-start.8 = (bf16[192,384]{1,0:T(8,128)(2,1)S(1)}, bf16[192,384]{1,0:T(8,128)(2,1)S(1)}, u32[]{:S(2)}, u32[]{:S(2)}) collective-permute-start(bf16[192,384]{1,0:T(8,128)(2,1)S(1)} %copy-done.33), channel_id=1, source_target_pairs={{0,1},{1,0},{2,3},{3,2},{4,5},{5,4},{6,7},{7,6},{8,9},{9,8},{10,11... | collective-permute-start | bytes 442376 | tf_op jit(solution)/shard_map/ppermute | solution.py:757
  31.4 15.3 %collective-permute-start.9 = (f32[2,192]{1,0:T(2,128)S(1)}, f32[2,192]{1,0:T(2,128)S(1)}, u32[]{:S(2)}, u32[]{:S(2)}) collective-permute-start(f32[2,192]{1,0:T(2,128)S(1)} %copy-done.48), channel_id=1, source_target_pairs={{0,1},{1,0},{2,3},{3,2},{4,5},{5,4},{6,7},{7,6},{8,9},{9,8},{10,11... | collective-permute-start | bytes 4616 | tf_op jit(solution)/shard_map/ppermute | solution.py:757
  31.8 38.4 %collective-permute-start.11 = (f32[1,768]{1,0:T(1,128)S(1)}, f32[1,768]{1,0:T(1,128)S(1)}, u32[]{:S(2)}, u32[]{:S(2)}) collective-permute-start(f32[1,768]{1,0:T(1,128)S(1)} %reshape.71.own_b1), channel_id=1, source_target_pairs={{0,1},{1,0},{2,3},{3,2},{4,5},{5,4},{6,7},{7,6},{8,9},{9,8},{10,11... | collective-permute-start | bytes 9224 | tf_op jit(solution)/shard_map/ppermute | solution.py:757
  165.7 2.5 collective-permute-start.15
  165.9 7.1 %collective-permute-start.30 = (bf16[1024,384]{1,0:T(8,128)(2,1)}, bf16[1024,384]{1,0:T(8,128)(2,1)S(1)}, u32[]{:S(2)}, u32[]{:S(2)}) collective-permute-start(bf16[1024,384]{1,0:T(8,128)(2,1)} %get-tuple-element.133), channel_id=1, source_target_pairs={{0,1},{1,0},{2,3},{3,2},{4,5},{5,4},{6,7},{7,6},{8,9},{9,8},{10,11... | collective-permute-start | bytes 2359304 | tf_op jit(solution)/shard_map/ppermute | solution.py:757
  166.2 28.6 %collective-permute-start.37 = (bf16[1536,384]{1,0:T(8,128)(2,1)}, bf16[1536,384]{1,0:T(8,128)(2,1)S(1)}, u32[]{:S(2)}, u32[]{:S(2)}) collective-permute-start(bf16[1536,384]{1,0:T(8,128)(2,1)} %get-tuple-element.142), channel_id=1, source_target_pairs={{0,1},{1,0},{2,3},{3,2},{4,5},{5,4},{6,7},{7,6},{8,9},{9,8},{10,11... | collective-permute-start | bytes 3538952 | tf_op jit(solution)/shard_map/ppermute | solution.py:757
  166.4 38.9 %collective-permute-start.22 = (bf16[1536,384]{1,0:T(8,128)(2,1)}, bf16[1536,384]{1,0:T(8,128)(2,1)S(1)}, u32[]{:S(2)}, u32[]{:S(2)}) collective-permute-start(bf16[1536,384]{1,0:T(8,128)(2,1)} %get-tuple-element.125), channel_id=1, source_target_pairs={{0,1},{1,0},{2,3},{3,2},{4,5},{5,4},{6,7},{7,6},{8,9},{9,8},{10,11... | collective-permute-start | bytes 3538952 | tf_op jit(solution)/shard_map/ppermute | solution.py:757
  170.3 7.8 %collective-permute-start.16 = (bf16[416,384]{1,0:T(8,128)(2,1)}, bf16[416,384]{1,0:T(8,128)(2,1)S(1)}, u32[]{:S(2)}, u32[]{:S(2)}) collective-permute-start(bf16[416,384]{1,0:T(8,128)(2,1)} %get-tuple-element.118), channel_id=1, source_target_pairs={{0,2},{1,5},{2,0},{3,7},{4,6},{5,1},{6,4},{7,3},{8,10},{9,13},{10,... | collective-permute-start | bytes 958472 | tf_op jit(solution)/shard_map/ppermute | solution.py:769
  176.2 14.5 %collective-permute-start.31 = (bf16[512,384]{1,0:T(8,128)(2,1)}, bf16[512,384]{1,0:T(8,128)(2,1)S(1)}, u32[]{:S(2)}, u32[]{:S(2)}) collective-permute-start(bf16[512,384]{1,0:T(8,128)(2,1)} %get-tuple-element.135), channel_id=1, source_target_pairs={{0,2},{1,5},{2,0},{3,7},{4,6},{5,1},{6,4},{7,3},{8,10},{9,13},{10,... | collective-permute-start | bytes 1179656 | tf_op jit(solution)/shard_map/ppermute | solution.py:769
  180.7 5.5 %collective-permute-start.17 = (bf16[208,384]{1,0:T(8,128)(2,1)}, bf16[208,384]{1,0:T(8,128)(2,1)S(1)}, u32[]{:S(2)}, u32[]{:S(2)}) collective-permute-start(bf16[208,384]{1,0:T(8,128)(2,1)} %get-tuple-element.120), channel_id=1, source_target_pairs={{0,4},{1,3},{2,6},{3,1},{4,0},{5,7},{6,2},{7,5},{8,12},{9,11},{10,... | collective-permute-start | bytes 479240 | tf_op jit(solution)/shard_map/ppermute | solution.py:769
  188.6 11.7 %collective-permute-start.18 = (bf16[208,384]{1,0:T(8,128)(2,1)}, bf16[208,384]{1,0:T(8,128)(2,1)S(1)}, u32[]{:S(2)}, u32[]{:S(2)}) collective-permute-start(bf16[208,384]{1,0:T(8,128)(2,1)} %add.34.mine), channel_id=1, source_target_pairs={{0,8},{1,17},{2,10},{3,19},{4,12},{5,21},{6,14},{7,23},{8,0},{9,25... | collective-permute-start | bytes 479240 | tf_op jit(solution)/shard_map/ppermute | solution.py:769
  193.3 15.8 %collective-permute-start.32 = (bf16[256,384]{1,0:T(8,128)(2,1)}, bf16[256,384]{1,0:T(8,128)(2,1)S(1)}, u32[]{:S(2)}, u32[]{:S(2)}) collective-permute-start(bf16[256,384]{1,0:T(8,128)(2,1)} %get-tuple-element.137), channel_id=1, source_target_pairs={{0,4},{1,3},{2,6},{3,1},{4,0},{5,7},{6,2},{7,5},{8,12},{9,11},{10,... | collective-permute-start | bytes 589832 | tf_op jit(solution)/shard_map/ppermute | solution.py:769
  195.9 9.4 %copy-start = (f32[784,384]{1,0:T(8,128)S(1)}, f32[784,384]{1,0:T(8,128)}, u32[]{:S(2)}) copy-start(f32[784,384]{1,0:T(8,128)} %get-tuple-element.114) | copy-start | bytes 3612676
  195.9 9.4 %copy-start.6 = (bf16[784,384]{1,0:T(8,128)(2,1)S(1)}, bf16[784,384]{1,0:T(8,128)(2,1)}, u32[]{:S(2)}) copy-start(bf16[784,384]{1,0:T(8,128)(2,1)} %get-tuple-element.89) | copy-start | bytes 1806340
  198.8 22.6 %collective-permute-start.38 = (bf16[768,384]{1,0:T(8,128)(2,1)}, bf16[768,384]{1,0:T(8,128)(2,1)S(1)}, u32[]{:S(2)}, u32[]{:S(2)}) collective-permute-start(bf16[768,384]{1,0:T(8,128)(2,1)} %get-tuple-element.144), channel_id=1, source_target_pairs={{0,2},{1,5},{2,0},{3,7},{4,6},{5,1},{6,4},{7,3},{8,10},{9,13},{10,... | collective-permute-start | bytes 1769480 | tf_op jit(solution)/shard_map/ppermute | solution.py:769
  202.7 8.9 %collective-permute-start.19 = (bf16[208,384]{1,0:T(8,128)(2,1)}, bf16[208,384]{1,0:T(8,128)(2,1)S(1)}, u32[]{:S(2)}, u32[]{:S(2)}) collective-permute-start(bf16[208,384]{1,0:T(8,128)(2,1)} %add.35.mine), channel_id=1, source_target_pairs={{0,16},{1,9},{2,18},{3,11},{4,20},{5,13},{6,22},{7,15},{8,24},{9,1... | collective-permute-start | bytes 479240 | tf_op jit(solution)/shard_map/ppermute | solution.py:769
  205.3 49.9 %collective-permute-start.14 = (f32[784,384]{1,0:T(8,128)S(1)}, f32[784,384]{1,0:T(8,128)S(1)}, u32[]{:S(2)}, u32[]{:S(2)}) collective-permute-start(f32[784,384]{1,0:T(8,128)S(1)} %copy-done), channel_id=1, source_target_pairs={{0,1},{1,0},{2,3},{3,2},{4,5},{5,4},{6,7},{7,6},{8,9},{9,8},{10,11... | collective-permute-start | bytes 3612680 | tf_op jit(solution)/shard_map/ppermute | solution.py:757
  205.3 24.1 %collective-permute-start.13 = (bf16[784,384]{1,0:T(8,128)(2,1)S(1)}, bf16[784,384]{1,0:T(8,128)(2,1)S(1)}, u32[]{:S(2)}, u32[]{:S(2)}) collective-permute-start(bf16[784,384]{1,0:T(8,128)(2,1)S(1)} %copy-done.6), channel_id=1, source_target_pairs={{0,1},{1,0},{2,3},{3,2},{4,5},{5,4},{6,7},{7,6},{8,9},{9,8},{10,11... | collective-permute-start | bytes 1806344 | tf_op jit(solution)/shard_map/ppermute | solution.py:757
  206.3 12.8 %copy-start.5 = (bf16[784,384]{1,0:T(8,128)(2,1)S(1)}, bf16[784,384]{1,0:T(8,128)(2,1)}, u32[]{:S(2)}) copy-start(bf16[784,384]{1,0:T(8,128)(2,1)} %get-tuple-element.86) | copy-start | bytes 1806340
  209.1 17.3 %collective-permute-start.23 = (bf16[768,384]{1,0:T(8,128)(2,1)}, bf16[768,384]{1,0:T(8,128)(2,1)S(1)}, u32[]{:S(2)}, u32[]{:S(2)}) collective-permute-start(bf16[768,384]{1,0:T(8,128)(2,1)} %get-tuple-element.127), channel_id=1, source_target_pairs={{0,2},{1,5},{2,0},{3,7},{4,6},{5,1},{6,4},{7,3},{8,10},{9,13},{10,... | collective-permute-start | bytes 1769480 | tf_op jit(solution)/shard_map/ppermute | solution.py:769
  211.6 8.2 %copy-start.29 = (bf16[208,384]{1,0:T(8,128)(2,1)}, bf16[208,384]{1,0:T(8,128)(2,1)S(1)}, u32[]{:S(2)}) copy-start(bf16[208,384]{1,0:T(8,128)(2,1)S(1)} %collective-permute-done.19.got) | copy-start | bytes 479236
  211.6 7.5 %collective-permute-start.33 = (bf16[256,384]{1,0:T(8,128)(2,1)}, bf16[256,384]{1,0:T(8,128)(2,1)S(1)}, u32[]{:S(2)}, u32[]{:S(2)}) collective-permute-start(bf16[256,384]{1,0:T(8,128)(2,1)} %add.40.mine), channel_id=1, source_target_pairs={{0,8},{1,17},{2,10},{3,19},{4,12},{5,21},{6,14},{7,23},{8,0},{9,25... | collective-permute-start | bytes 589832 | tf_op jit(solution)/shard_map/ppermute | solution.py:769
  219.1 3.5 %copy-start.27 = (bf16[256,384]{1,0:T(8,128)(2,1)}, bf16[256,384]{1,0:T(8,128)(2,1)S(1)}, u32[]{:S(2)}) copy-start(bf16[256,384]{1,0:T(8,128)(2,1)S(1)} %collective-permute-done.33.got) | copy-start | bytes 589828
  219.1 18.5 %collective-permute-start.6 = (bf16[784,384]{1,0:T(8,128)(2,1)S(1)}, bf16[784,384]{1,0:T(8,128)(2,1)S(1)}, u32[]{:S(2)}, u32[]{:S(2)}) collective-permute-start(bf16[784,384]{1,0:T(8,128)(2,1)S(1)} %copy-done.5), channel_id=1, source_target_pairs={{0,1},{1,0},{2,3},{3,2},{4,5},{5,4},{6,7},{7,6},{8,9},{9,8},{10,11... | collective-permute-start | bytes 1806344 | tf_op jit(solution)/shard_map/ppermute | solution.py:757
  221.4 8.9 %collective-permute-start.20 = (bf16[208,384]{1,0:T(8,128)(2,1)}, bf16[208,384]{1,0:T(8,128)(2,1)S(1)}, u32[]{:S(2)}, u32[]{:S(2)}) collective-permute-start(bf16[208,384]{1,0:T(8,128)(2,1)} %add.36.mine), channel_id=1, source_target_pairs={{0,4},{1,3},{2,6},{3,1},{4,0},{5,7},{6,2},{7,5},{8,12},{9,11},{10,... | collective-permute-start | bytes 479240 | tf_op jit(solution)/shard_map/ppermute | solution.py:769
  226.5 8.5 %collective-permute-start.34 = (bf16[256,384]{1,0:T(8,128)(2,1)}, bf16[256,384]{1,0:T(8,128)(2,1)S(1)}, u32[]{:S(2)}, u32[]{:S(2)}) collective-permute-start(bf16[256,384]{1,0:T(8,128)(2,1)} %add.41.mine), channel_id=1, source_target_pairs={{0,16},{1,9},{2,18},{3,11},{4,20},{5,13},{6,22},{7,15},{8,24},{9,1... | collective-permute-start | bytes 589832 | tf_op jit(solution)/shard_map/ppermute | solution.py:769
  229.4 18.6 %collective-permute-start.39 = (bf16[384,384]{1,0:T(8,128)(2,1)}, bf16[384,384]{1,0:T(8,128)(2,1)S(1)}, u32[]{:S(2)}, u32[]{:S(2)}) collective-permute-start(bf16[384,384]{1,0:T(8,128)(2,1)} %get-tuple-element.146), channel_id=1, source_target_pairs={{0,4},{1,3},{2,6},{3,1},{4,0},{5,7},{6,2},{7,5},{8,12},{9,11},{10,... | collective-permute-start | bytes 884744 | tf_op jit(solution)/shard_map/ppermute | solution.py:769
  230.3 20.6 %collective-permute-start.24 = (bf16[384,384]{1,0:T(8,128)(2,1)}, bf16[384,384]{1,0:T(8,128)(2,1)S(1)}, u32[]{:S(2)}, u32[]{:S(2)}) collective-permute-start(bf16[384,384]{1,0:T(8,128)(2,1)} %get-tuple-element.129), channel_id=1, source_target_pairs={{0,4},{1,3},{2,6},{3,1},{4,0},{5,7},{6,2},{7,5},{8,12},{9,11},{10,... | collective-permute-start | bytes 884744 | tf_op jit(solution)/shard_map/ppermute | solution.py:769
  235.0 21.8 %collective-permute-start.21 = (bf16[416,384]{1,0:T(8,128)(2,1)}, bf16[416,384]{1,0:T(8,128)(2,1)S(1)}, u32[]{:S(2)}, u32[]{:S(2)}) collective-permute-start(bf16[416,384]{1,0:T(8,128)(2,1)} %join.4.mine), channel_id=1, source_target_pairs={{0,2},{1,5},{2,0},{3,7},{4,6},{5,1},{6,4},{7,3},{8,10},{9,13},{10,... | collective-permute-start | bytes 958472 | tf_op jit(solution)/shard_map/ppermute | solution.py:769
  237.6 7.5 %collective-permute-start.35 = (bf16[256,384]{1,0:T(8,128)(2,1)}, bf16[256,384]{1,0:T(8,128)(2,1)S(1)}, u32[]{:S(2)}, u32[]{:S(2)}) collective-permute-start(bf16[256,384]{1,0:T(8,128)(2,1)} %add.42.mine), channel_id=1, source_target_pairs={{0,4},{1,3},{2,6},{3,1},{4,0},{5,7},{6,2},{7,5},{8,12},{9,11},{10,... | collective-permute-start | bytes 589832 | tf_op jit(solution)/shard_map/ppermute | solution.py:769
  247.5 24.9 %collective-permute-start.36 = (bf16[512,384]{1,0:T(8,128)(2,1)}, bf16[512,384]{1,0:T(8,128)(2,1)S(1)}, u32[]{:S(2)}, u32[]{:S(2)}) collective-permute-start(bf16[512,384]{1,0:T(8,128)(2,1)} %join.6.mine), channel_id=1, source_target_pairs={{0,2},{1,5},{2,0},{3,7},{4,6},{5,1},{6,4},{7,3},{8,10},{9,13},{10,... | collective-permute-start | bytes 1179656 | tf_op jit(solution)/shard_map/ppermute | solution.py:769
  250.6 13.1 %collective-permute-start.40 = (bf16[384,384]{1,0:T(8,128)(2,1)}, bf16[384,384]{1,0:T(8,128)(2,1)S(1)}, u32[]{:S(2)}, u32[]{:S(2)}) collective-permute-start(bf16[384,384]{1,0:T(8,128)(2,1)} %add.43.mine), channel_id=1, source_target_pairs={{0,8},{1,17},{2,10},{3,19},{4,12},{5,21},{6,14},{7,23},{8,0},{9,25... | collective-permute-start | bytes 884744 | tf_op jit(solution)/shard_map/ppermute | solution.py:769
  253.5 15.0 %collective-permute-start.25 = (bf16[384,384]{1,0:T(8,128)(2,1)}, bf16[384,384]{1,0:T(8,128)(2,1)S(1)}, u32[]{:S(2)}, u32[]{:S(2)}) collective-permute-start(bf16[384,384]{1,0:T(8,128)(2,1)} %add.37.mine), channel_id=1, source_target_pairs={{0,8},{1,17},{2,10},{3,19},{4,12},{5,21},{6,14},{7,23},{8,0},{9,25... | collective-permute-start | bytes 884744 | tf_op jit(solution)/shard_map/ppermute | solution.py:769
  259.9 15.9 %collective-permute-start.29 = (f32[64,384]{1,0:T(8,128)}, f32[64,384]{1,0:T(8,128)S(1)}, u32[]{:S(2)}, u32[]{:S(2)}) collective-permute-start(f32[64,384]{1,0:T(8,128)} %get-tuple-element.122), channel_id=1, source_target_pairs={{0,1},{1,0},{2,3},{3,2},{4,5},{5,4},{6,7},{7,6},{8,9},{9,8},{10,11... | collective-permute-start | bytes 294920 | tf_op jit(solution)/shard_map/ppermute | solution.py:757
  263.1 8.6 %copy-start.35 = (f32[64,384]{1,0:T(8,128)S(1)}, f32[64,384]{1,0:T(8,128)}, u32[]{:S(2)}) copy-start(f32[64,384]{1,0:T(8,128)} %get-tuple-element.122) | copy-start | bytes 294916
  266.3 11.1 %collective-permute-start.41 = (bf16[384,384]{1,0:T(8,128)(2,1)}, bf16[384,384]{1,0:T(8,128)(2,1)S(1)}, u32[]{:S(2)}, u32[]{:S(2)}) collective-permute-start(bf16[384,384]{1,0:T(8,128)(2,1)} %add.44.mine), channel_id=1, source_target_pairs={{0,16},{1,9},{2,18},{3,11},{4,20},{5,13},{6,22},{7,15},{8,24},{9,1... | collective-permute-start | bytes 884744 | tf_op jit(solution)/shard_map/ppermute | solution.py:769
  271.0 12.4 %collective-permute-start.26 = (bf16[384,384]{1,0:T(8,128)(2,1)}, bf16[384,384]{1,0:T(8,128)(2,1)S(1)}, u32[]{:S(2)}, u32[]{:S(2)}) collective-permute-start(bf16[384,384]{1,0:T(8,128)(2,1)} %add.38.mine), channel_id=1, source_target_pairs={{0,16},{1,9},{2,18},{3,11},{4,20},{5,13},{6,22},{7,15},{8,24},{9,1... | collective-permute-start | bytes 884744 | tf_op jit(solution)/shard_map/ppermute | solution.py:769
  275.7 12.0 %copy-start.12 = (f32[256,384]{1,0:T(8,128)S(1)}, f32[256,384]{1,0:T(8,128)}, u32[]{:S(2)}) copy-start(f32[256,384]{1,0:T(8,128)} %get-tuple-element.139) | copy-start | bytes 1179652
  275.8 12.0 %copy-start.3 = (f32[3,384,192]{2,1,0:T(8,128)S(1)}, f32[3,384,192]{2,1,0:T(8,128)}, u32[]{:S(2)}) copy-start(f32[3,384,192]{2,1,0:T(8,128)} %get-tuple-element.202) | copy-start | bytes 2654212
  275.8 21.9 %collective-permute-start.44 = (f32[256,384]{1,0:T(8,128)}, f32[256,384]{1,0:T(8,128)S(1)}, u32[]{:S(2)}, u32[]{:S(2)}) collective-permute-start(f32[256,384]{1,0:T(8,128)} %get-tuple-element.139), channel_id=1, source_target_pairs={{0,1},{1,0},{2,3},{3,2},{4,5},{5,4},{6,7},{7,6},{8,9},{9,8},{10,11... | collective-permute-start | bytes 1179656 | tf_op jit(solution)/shard_map/ppermute | solution.py:757
  280.0 10.3 %collective-permute-start.42 = (bf16[384,384]{1,0:T(8,128)(2,1)}, bf16[384,384]{1,0:T(8,128)(2,1)S(1)}, u32[]{:S(2)}, u32[]{:S(2)}) collective-permute-start(bf16[384,384]{1,0:T(8,128)(2,1)} %add.45.mine), channel_id=1, source_target_pairs={{0,4},{1,3},{2,6},{3,1},{4,0},{5,7},{6,2},{7,5},{8,12},{9,11},{10,... | collective-permute-start | bytes 884744 | tf_op jit(solution)/shard_map/ppermute | solution.py:769
  285.9 8.3 %collective-permute-start.27 = (bf16[384,384]{1,0:T(8,128)(2,1)}, bf16[384,384]{1,0:T(8,128)(2,1)S(1)}, u32[]{:S(2)}, u32[]{:S(2)}) collective-permute-start(bf16[384,384]{1,0:T(8,128)(2,1)} %add.39.mine), channel_id=1, source_target_pairs={{0,4},{1,3},{2,6},{3,1},{4,0},{5,7},{6,2},{7,5},{8,12},{9,11},{10,... | collective-permute-start | bytes 884744 | tf_op jit(solution)/shard_map/ppermute | solution.py:769
  293.0 10.1 %collective-permute-start.43 = (bf16[768,384]{1,0:T(8,128)(2,1)}, bf16[768,384]{1,0:T(8,128)(2,1)S(1)}, u32[]{:S(2)}, u32[]{:S(2)}) collective-permute-start(bf16[768,384]{1,0:T(8,128)(2,1)} %join.7.mine), channel_id=1, source_target_pairs={{0,2},{1,5},{2,0},{3,7},{4,6},{5,1},{6,4},{7,3},{8,10},{9,13},{10,... | collective-permute-start | bytes 1769480 | tf_op jit(solution)/shard_map/ppermute | solution.py:769
  296.8 12.5 %collective-permute-start.28 = (bf16[768,384]{1,0:T(8,128)(2,1)}, bf16[768,384]{1,0:T(8,128)(2,1)S(1)}, u32[]{:S(2)}, u32[]{:S(2)}) collective-permute-start(bf16[768,384]{1,0:T(8,128)(2,1)} %join.5.mine), channel_id=1, source_target_pairs={{0,2},{1,5},{2,0},{3,7},{4,6},{5,1},{6,4},{7,3},{8,10},{9,13},{10,... | collective-permute-start | bytes 1769480 | tf_op jit(solution)/shard_map/ppermute | solution.py:769
  (32 other events, 28.3 us)
